TPU v7x, 256 devices: a whole 4x4x8 slice. The times are simulated.
256 devices in a mesh: tm: 8 (over x_lo, y), rows: 32 (over z, x_hi, core).
Axes of the slice: x: 4 (x_hi: 2, x_lo: 2; x = x_hi * 2 + x_lo), y: 4, z: 8, core: 2. Of those that a mesh axis runs over, the one named last changes fastest.
Arguments:
- video_in: bfloat16 [16, 32, 192, 128], P('tm', 'rows'), may hold values from -6 to 6
- kernels: bfloat16 [2, 5184, 192], replicated, may hold values from -0.15625 to 0.15625
- cotangent: bfloat16 [16, 32, 192, 128], P('tm', 'rows'), may hold values from -6 to 6
Outputs:
- input_grad: bfloat16 [16, 32, 192, 128], P('tm', 'rows')
- kernel_grad: float32 [2, 5184, 192], P(None, 'rows')
All inputs are finite; a program needn't handle non-finite values.
Results may differ from a plain program's by a relative error of at most 0.01.
Values may be sent and summed in bfloat16 or wider, within the bound.
A program may use at most 128 MiB of HBM per device.

v0:
```python
import math

import jax
import jax.numpy as jnp
from jax import lax
from jax.sharding import PartitionSpec as P


def from_behind(value, axis, steps):
    count = lax.axis_size(axis)
    initial, last = (max(0, -steps), min(count, count - steps))
    return lax.ppermute(value, axis, [(source, source + steps) for source in range(initial, last)])


def padded(value, sides, width):
    for axis, dim in sides:
        peers, length = (lax.axis_size(axis), value.shape[dim])
        up = [(i, (i + 1) % peers) for i in range(peers - 1)]
        down = [(j, i) for i, j in up]
        last = lax.slice_in_dim(value, length - width, length, axis=dim)
        initial = lax.slice_in_dim(value, 0, width, axis=dim)
        before = lax.ppermute(last, axis, up)
        after = lax.ppermute(initial, axis, down)
        value = jnp.concatenate([before, value, after], axis=dim)
    return value


def stacked_taps(extended, frame_count, row_count, col_count, flipped):
    pieces = []
    for time_tap in range(3):
        for row_tap in range(3):
            for col_tap in range(3):
                if flipped:
                    time_at, row_at, col_at = (2 - time_tap, 2 - row_tap, 2 - col_tap)
                else:
                    time_at, row_at, col_at = (time_tap, row_tap, col_tap)
                pieces.append(
                    extended[
                        time_at : time_at + frame_count,
                        row_at : row_at + row_count,
                        :,
                        col_at : col_at + col_count,
                    ]
                )
    return jnp.concatenate(pieces, axis=2)


def extend_past(acts):
    earlier = from_behind(acts, "tm", 1)
    extended = jnp.concatenate([earlier, acts], axis=0)
    extended = padded(extended, (("rows", 1),), 1)
    return jnp.pad(extended, ((0, 0), (0, 0), (0, 0), (1, 1)))


def extend_future(grad):
    later = from_behind(grad, "tm", -1)
    extended = jnp.concatenate([grad, later], axis=0)
    extended = padded(extended, (("rows", 1),), 1)
    return jnp.pad(extended, ((0, 0), (0, 0), (0, 0), (1, 1)))


def on_device(video_in, kernels, cotangent):
    frame_count, row_count, channel, col_count = video_in.shape
    layer_count = kernels.shape[0]
    saved_inputs = []
    saved_columns = []
    state = video_in
    for layer_id in range(layer_count):
        acts = jax.nn.silu(state.astype(jnp.float32)).astype(jnp.bfloat16)
        columns = stacked_taps(extend_past(acts), frame_count, row_count, col_count, False)
        saved_inputs.append(state)
        saved_columns.append(columns)
        state = jnp.einsum(
            "frkw,kd->frdw", columns, kernels[layer_id], preferred_element_type=jnp.float32
        ).astype(jnp.bfloat16)
    grad = cotangent
    local_terms = [None] * layer_count
    for layer_id in reversed(range(layer_count)):
        partial_grad = jnp.einsum(
            "frkw,frdw->kd", saved_columns[layer_id], grad, preferred_element_type=jnp.float32
        )
        local_terms[layer_id] = partial_grad
        flipped_kernel = (
            kernels[layer_id]
            .reshape(27, channel, channel)
            .transpose(1, 0, 2)
            .reshape(channel, 27 * channel)
        )
        grad_columns = stacked_taps(extend_future(grad), frame_count, row_count, col_count, True)
        back = jnp.einsum(
            "frkw,ck->frcw", grad_columns, flipped_kernel, preferred_element_type=jnp.float32
        )
        wide_in = saved_inputs[layer_id].astype(jnp.float32)
        sigma = jax.nn.sigmoid(wide_in)
        grad = (back * sigma * (1.0 + wide_in * (1.0 - sigma))).astype(jnp.bfloat16)
    share = lax.psum_scatter(jnp.stack(local_terms), "rows", scatter_dimension=1, tiled=True)
    summed = lax.psum(share, "tm")
    total_cells = frame_count * lax.axis_size("tm") * row_count * lax.axis_size("rows") * col_count
    scale_factor = 1.0 / math.sqrt(total_cells)
    return (grad, summed * scale_factor)


def solution(mesh):
    return jax.shard_map(
        on_device,
        mesh=mesh,
        in_specs=(P("tm", "rows", None, None), P(), P("tm", "rows", None, None)),
        out_specs=(P("tm", "rows", None, None), P(None, "rows", None)),
        check_vma=False,
    )
```

profile of v0, /device:TPU:2, one launch (start us, length us, event | category | flops | bytes accessed | tf_op | source)
XLA Modules:
  0.0 490.5 jit_solution(11184660338216132403)
XLA Ops:
  7.2 4.9 collective-permute-start
  13.1 1.9 collective-permute-start.3
  15.0 1.6 pad_maximum_fusion.1
  17.9 3.0 collective-permute-start.1
  20.9 4.4 fusion.81
  25.3 3.8 copy.41
  29.2 3.4 copy.29
  32.6 1.3 collective-permute-start.5
  33.9 4.8 collective-permute-start.4
  44.4 2.4 collective-permute-start.9
  47.8 5.6 %collective-permute-done.9 = bf16[2,1,192,128]{3,2,0,1:T(8,128)(2,1)S(1)} collective-permute-done((bf16[2,1,192,128]{3,2,0,1:T(8,128)(2,1)S(1)}, bf16[2,1,192,128]{3,2,0,1:T(8,128)(2,1)S(1)}, u32[]{:S(2)}, u32[]{:S(2)}) %collective-permute-start.9) | collective-permute-done | bytes 98336 | tf_op jit(solution)/shard_map/ppermute | solution.py:12
  54.8 6.8 %collective-permute-start.10 = (bf16[4,1,192,128]{3,2,0,1:T(8,128)(2,1)S(1)}, bf16[4,1,192,128]{3,2,0,1:T(8,128)(2,1)S(1)}, u32[]{:S(2)}, u32[]{:S(2)}) collective-permute-start(bf16[4,1,192,128]{3,2,0,1:T(8,128)(2,1)S(1)} %pad_maximum_fusion.4), channel_id=1, source_target_pairs={{0,1},{1,2},{2,3},{3,4},{4,5},{5,6},{6,7},{7,8},{8,9},{9,10},{10,1... | collective-permute-start | bytes 589832 | tf_op jit(solution)/shard_map/ppermute | solution.py:22
  65.8 3.8 pad_maximum_fusion
  69.5 16.1 %copy.35 = f32[2,5184,192]{2,0,1:T(2,128)} copy(f32[2,5184,192]{1,2,0:T(8,128)} %pad_maximum_fusion) | data formatting | bytes 15925248 | tf_op jit(solution)/shard_map/stack | solution.py:96
  85.7 3.6 collective-permute-start.6
  89.4 2.9 collective-permute-done.6
  93.6 8.8 %collective-permute-start.7 = (bf16[4,1,192,128]{3,2,0,1:T(8,128)(2,1)S(1)}, bf16[4,1,192,128]{3,2,0,1:T(8,128)(2,1)S(1)}, u32[]{:S(2)}, u32[]{:S(2)}) collective-permute-start(bf16[4,1,192,128]{3,2,0,1:T(8,128)(2,1)S(1)} %pad_maximum_fusion.3), channel_id=1, source_target_pairs={{0,1},{1,2},{2,3},{3,4},{4,5},{5,6},{6,7},{7,8},{8,9},{9,10},{10,1... | collective-permute-start | bytes 589832 | tf_op jit(solution)/shard_map/ppermute | solution.py:22
  102.4 3.9 copy.32
  106.3 3.4 copy.33
  129.9 270.6 %all-reduce.10.cloned.1.call-done = f32[2,5184,192]{2,0,1:T(2,128)} async-done(((f32[2,5184,192]{2,0,1:T(2,128)}), f32[2,5184,192]{2,0,1:T(2,128)}) %all-reduce.10.cloned.1.call-update) | async-done | bytes 7962640
  400.5 1.8 constant_dynamic-slice_fusion
  402.4 3.5 fusion.66
  405.8 76.0 %all-reduce.8.cloned.1.call-done = f32[2,162,192]{2,0,1:T(2,128)} async-done(((f32[2,162,192]{2,0,1:T(2,128)}), f32[2,162,192]{2,0,1:T(2,128)}) %all-reduce.8.cloned.1.call-update) | async-done | bytes 248848 | tf_op jit(solution)/shard_map/psum | solution.py:97
  481.8 1.8 broadcast_multiply_fusion
  (150 shorter events, 34.8 us)
Async XLA Ops:
  7.2 393.4 %all-reduce.10.cloned.1.call-start = ((), (), s32[]{:S(2)}) async-start(), calls=%async_computation.1 | async-start | bytes 21233664
  7.2 7.8 %collective-permute-start = (bf16[2,1,192,128]{3,2,0,1:T(8,128)(2,1)}, bf16[2,1,192,128]{3,2,0,1:T(8,128)(2,1)S(1)}, u32[]{:S(2)}, u32[]{:S(2)}) collective-permute-start(bf16[2,1,192,128]{3,2,0,1:T(8,128)(2,1)} %bitcast.126), channel_id=1, source_target_pairs={{32,0},{64,32},{96,64},{128,96},{160,128},{192,160},{224,192},{33,... | collective-permute-start | bytes 294920 | tf_op jit(solution)/shard_map/ppermute | solution.py:12
  13.1 19.5 %collective-permute-start.3 = (bf16[2,1,192,128]{3,2,0,1:T(8,128)(2,1)S(1)}, bf16[2,1,192,128]{3,2,0,1:T(8,128)(2,1)S(1)}, u32[]{:S(2)}, u32[]{:S(2)}) collective-permute-start(bf16[2,1,192,128]{3,2,0,1:T(8,128)(2,1)S(1)} %fusion.72), channel_id=1, source_target_pairs={{0,32},{32,64},{64,96},{96,128},{128,160},{160,192},{192,224},{1,3... | collective-permute-start | bytes 294920 | tf_op jit(solution)/shard_map/ppermute | solution.py:12
  16.6 22.2 %collective-permute-start.2 = (bf16[4,1,192,128]{3,2,0,1:T(8,128)(2,1)}, bf16[4,1,192,128]{3,2,0,1:T(8,128)(2,1)S(1)}, u32[]{:S(2)}, u32[]{:S(2)}) collective-permute-start(bf16[4,1,192,128]{3,2,0,1:T(8,128)(2,1)} %pad_maximum_fusion.1), channel_id=1, source_target_pairs={{1,0},{2,1},{3,2},{4,3},{5,4},{6,5},{7,6},{8,7},{9,8},{10,9},{11,1... | collective-permute-start | bytes 589832 | tf_op jit(solution)/shard_map/ppermute | solution.py:23
  17.9 20.9 %collective-permute-start.1 = (bf16[4,1,192,128]{3,2,0,1:T(8,128)(2,1)}, bf16[4,1,192,128]{3,2,0,1:T(8,128)(2,1)S(1)}, u32[]{:S(2)}, u32[]{:S(2)}) collective-permute-start(bf16[4,1,192,128]{3,2,0,1:T(8,128)(2,1)} %pad_maximum_fusion.1), channel_id=1, source_target_pairs={{0,1},{1,2},{2,3},{3,4},{4,5},{5,6},{6,7},{7,8},{8,9},{9,10},{10,1... | collective-permute-start | bytes 589832 | tf_op jit(solution)/shard_map/ppermute | solution.py:22
  29.2 9.6 %copy-start.3 = (bf16[2,1,192,128]{3,2,1,0:T(8,128)(2,1)S(1)}, bf16[2,1,192,128]{3,2,1,0:T(8,128)(2,1)}, u32[]{:S(2)}) copy-start(bf16[2,1,192,128]{3,2,1,0:T(8,128)(2,1)} %param.5) | copy-start | bytes 294916
  32.6 8.2 %collective-permute-start.5 = (bf16[4,1,192,128]{3,2,0,1:T(8,128)(2,1)S(1)}, bf16[4,1,192,128]{3,2,0,1:T(8,128)(2,1)S(1)}, u32[]{:S(2)}, u32[]{:S(2)}) collective-permute-start(bf16[4,1,192,128]{3,2,0,1:T(8,128)(2,1)S(1)} %pad_maximum_fusion.2), channel_id=1, source_target_pairs={{1,0},{2,1},{3,2},{4,3},{5,4},{6,5},{7,6},{8,7},{9,8},{10,9},{11,1... | collective-permute-start | bytes 589832 | tf_op jit(solution)/shard_map/ppermute | solution.py:23
  33.9 6.9 %collective-permute-start.4 = (bf16[4,1,192,128]{3,2,0,1:T(8,128)(2,1)S(1)}, bf16[4,1,192,128]{3,2,0,1:T(8,128)(2,1)S(1)}, u32[]{:S(2)}, u32[]{:S(2)}) collective-permute-start(bf16[4,1,192,128]{3,2,0,1:T(8,128)(2,1)S(1)} %pad_maximum_fusion.2), channel_id=1, source_target_pairs={{0,1},{1,2},{2,3},{3,4},{4,5},{5,6},{6,7},{7,8},{8,9},{9,10},{10,1... | collective-permute-start | bytes 589832 | tf_op jit(solution)/shard_map/ppermute | solution.py:22
  40.8 1.8 copy-start.4
  41.5 2.2 copy-start
  43.6 3.1 copy-start.1
  44.4 9.1 %collective-permute-start.9 = (bf16[2,1,192,128]{3,2,0,1:T(8,128)(2,1)S(1)}, bf16[2,1,192,128]{3,2,0,1:T(8,128)(2,1)S(1)}, u32[]{:S(2)}, u32[]{:S(2)}) collective-permute-start(bf16[2,1,192,128]{3,2,0,1:T(8,128)(2,1)S(1)} %get-tuple-element.10), channel_id=1, source_target_pairs={{0,32},{32,64},{64,96},{96,128},{128,160},{160,192},{192,224},{1,3... | collective-permute-start | bytes 294920 | tf_op jit(solution)/shard_map/ppermute | solution.py:12
  53.5 9.2 %collective-permute-start.11 = (bf16[4,1,192,128]{3,2,0,1:T(8,128)(2,1)S(1)}, bf16[4,1,192,128]{3,2,0,1:T(8,128)(2,1)S(1)}, u32[]{:S(2)}, u32[]{:S(2)}) collective-permute-start(bf16[4,1,192,128]{3,2,0,1:T(8,128)(2,1)S(1)} %pad_maximum_fusion.4), channel_id=1, source_target_pairs={{1,0},{2,1},{3,2},{4,3},{5,4},{6,5},{7,6},{8,7},{9,8},{10,9},{11,1... | collective-permute-start | bytes 589832 | tf_op jit(solution)/shard_map/ppermute | solution.py:23
  54.8 7.9 %collective-permute-start.10 = (bf16[4,1,192,128]{3,2,0,1:T(8,128)(2,1)S(1)}, bf16[4,1,192,128]{3,2,0,1:T(8,128)(2,1)S(1)}, u32[]{:S(2)}, u32[]{:S(2)}) collective-permute-start(bf16[4,1,192,128]{3,2,0,1:T(8,128)(2,1)S(1)} %pad_maximum_fusion.4), channel_id=1, source_target_pairs={{0,1},{1,2},{2,3},{3,4},{4,5},{5,6},{6,7},{7,8},{8,9},{9,10},{10,1... | collective-permute-start | bytes 589832 | tf_op jit(solution)/shard_map/ppermute | solution.py:22
  85.7 396.1 %all-reduce.8.cloned.1.call-start = ((), (), s32[]{:S(2)}) async-start(), calls=%async_computation | async-start | bytes 663552 | tf_op jit(solution)/shard_map/psum | solution.py:97
  85.7 6.5 %collective-permute-start.6 = (bf16[2,1,192,128]{3,2,0,1:T(8,128)(2,1)S(1)}, bf16[2,1,192,128]{3,2,0,1:T(8,128)(2,1)S(1)}, u32[]{:S(2)}, u32[]{:S(2)}) collective-permute-start(bf16[2,1,192,128]{3,2,0,1:T(8,128)(2,1)S(1)} %fusion.45), channel_id=1, source_target_pairs={{32,0},{64,32},{96,64},{128,96},{160,128},{192,160},{224,192},{33,... | collective-permute-start | bytes 294920 | tf_op jit(solution)/shard_map/ppermute | solution.py:12
  92.3 18.7 %collective-permute-start.8 = (bf16[4,1,192,128]{3,2,0,1:T(8,128)(2,1)S(1)}, bf16[4,1,192,128]{3,2,0,1:T(8,128)(2,1)S(1)}, u32[]{:S(2)}, u32[]{:S(2)}) collective-permute-start(bf16[4,1,192,128]{3,2,0,1:T(8,128)(2,1)S(1)} %pad_maximum_fusion.3), channel_id=1, source_target_pairs={{1,0},{2,1},{3,2},{4,3},{5,4},{6,5},{7,6},{8,7},{9,8},{10,9},{11,1... | collective-permute-start | bytes 589832 | tf_op jit(solution)/shard_map/ppermute | solution.py:23
  93.6 17.4 %collective-permute-start.7 = (bf16[4,1,192,128]{3,2,0,1:T(8,128)(2,1)S(1)}, bf16[4,1,192,128]{3,2,0,1:T(8,128)(2,1)S(1)}, u32[]{:S(2)}, u32[]{:S(2)}) collective-permute-start(bf16[4,1,192,128]{3,2,0,1:T(8,128)(2,1)S(1)} %pad_maximum_fusion.3), channel_id=1, source_target_pairs={{0,1},{1,2},{2,3},{3,4},{4,5},{5,6},{6,7},{7,8},{8,9},{9,10},{10,1... | collective-permute-start | bytes 589832 | tf_op jit(solution)/shard_map/ppermute | solution.py:22
  106.3 3.4 copy-start.5
  115.6 286.7 %copy-start.2 = (bf16[192,27,192]{0,2,1:T(8,128)(2,1)S(1)}, bf16[192,27,192]{0,2,1:T(8,128)(2,1)}, u32[]{:S(2)}) copy-start(bf16[192,27,192]{0,2,1:T(8,128)(2,1)} %copy.33) | copy-start | bytes 5971972
Sparse Core Ops, SparseCore 0:
  85.8 314.6 all-reduce.9
  403.7 78.0 all-reduce.7
where the time goes:
time: 492 us; the launch traced here: 490 us
  waiting for transfers between devices  355 us (72%)
  local copies, waits for them, and re-layouts  59.7 us (12%)
  starting transfers between devices  41.6 us (8%)
  between operations  15.4 us (3%)
  other arithmetic  11.3 us (2%)
  matrix products  7.37 us (1%)
    unnamed x3, waiting for transfers between devices  271 us
    psum x1, waiting for transfers between devices, on_device(): summed = lax.psum(share, 'tm')  76 us
    unnamed x114, local copies, waits for them, and re-layouts  27.6 us
    ppermute x4, starting transfers between devices, padded(): before = lax.ppermute(last, axis, up)  23.5 us
    another operation x1, local copies, waits for them, and re-layouts, on_device(): jnp.stack(local_terms)  16.1 us
    ppermute x4, starting transfers between devices, from_behind(): lax.ppermute(value, axis, [(source, source + steps) for source in range(i...  12.8 us
  transfers between devices with their start and end apart: 14, of which 4 were waited for; matrix products, arithmetic and copies ran while one was open for 10% of the time, Pallas kernels for 0%

commit v1 on v0

v1 whole, which is shorter than its diff:
```python
import math

import jax
import jax.numpy as jnp
from jax import lax
from jax.experimental import pallas as pl
from jax.experimental.pallas import tpu as pltpu
from jax.sharding import PartitionSpec as P

MESH = pl.DeviceIdType.MESH
F32 = jnp.float32
BF16 = jnp.bfloat16
C = 192
W = 128
TM = 8
ROWS = 32
HALF = 2592
CHUNK = 176


def dot(a, b):
    return lax.dot_general(a, b, (((1,), (0,)), ((), ())), preferred_element_type=F32)


def dot_nt(a, b):
    return lax.dot_general(a, b, (((1,), (1,)), ((), ())), preferred_element_type=F32)


def lane_shift(value, by):
    rolled = pltpu.roll(value, by % W, 1)
    col = lax.broadcasted_iota(jnp.int32, value.shape, 1)
    edge = 0 if by == 1 else W - 1
    return jnp.where(col == edge, 0.0, rolled)


def sublane_shift(value, by):
    rolled = pltpu.roll(value, by % W, 0)
    row = lax.broadcasted_iota(jnp.int32, value.shape, 0)
    edge = 0 if by == 1 else W - 1
    return jnp.where(row == edge, 0.0, rolled)


def silu_parts(value):
    sigma = jax.nn.sigmoid(value)
    return value * sigma, sigma * (1.0 + value * (1.0 - sigma))


def group_a(y):
    return 16 * jnp.minimum(3 * y, 8)


def group_b(y):
    return 16 * (y + jnp.where(y >= 2, 1, 0))


def chunk_start(j):
    return pl.multiple_of(16 * ((81 * j) // 8), 16)


def kernel(
    video, kernels, cotangent, in_grad, k_grad,
    k1, k2, vext, cext, gext, acts, acts_t, acc_t, acc, x1, wa, wb, pair_in, summed,
    r1a, r1b, ta, tb, r2a, r2b, ub, r3, r4, final,
    load_sem, halo_send, halo_recv, pair_send, pair_recv,
    s1_send, s1_recv, s2_send, s2_recv, s3_send, s3_recv, s4_send, s4_recv,
):
    t = lax.axis_index("tm")
    r = lax.axis_index("rows")
    xl, y = t // 4, t % 4
    z, xh, c = r // 4, (r // 2) % 2, r % 2
    x = 2 * xh + xl
    has_up, has_down = r > 0, r < ROWS - 1
    has_past, has_future = t > 0, t < TM - 1

    loads = [
        pltpu.make_async_copy(video, vext.at[1, 1], load_sem.at[0]),
        pltpu.make_async_copy(cotangent, cext.at[0, 1], load_sem.at[1]),
        pltpu.make_async_copy(kernels.at[0], k1, load_sem.at[2]),
        pltpu.make_async_copy(kernels.at[1], k2, load_sem.at[3]),
    ]
    for load in loads:
        load.start()

    barrier = pltpu.get_barrier_semaphore()

    def greet(device):
        pl.semaphore_signal(barrier, inc=1, device_id=device, device_id_type=MESH)

    @pl.when(has_up)
    def _():
        greet((t, r - 1))

    @pl.when(has_down)
    def _():
        greet((t, r + 1))

    for e in range(1, 8):
        greet((lax.rem(t + e, 8), r))
        greet((t, lax.rem(z + e, 8) * 4 + xh * 2 + c))
    greet((xl * 4 + y, z * 4 + (1 - xh) * 2 + c))
    greet(((1 - xl) * 4 + y, z * 4 + (1 - xh) * 2 + c))

    neighbours = jnp.where(has_up, 1, 0) + jnp.where(has_down, 1, 0)
    pl.semaphore_wait(barrier, 16 + neighbours)

    exts = (vext, cext, gext)

    def own_of(field):
        return 1 if field == 0 else 0

    def side_of(field):
        return 0 if field == 0 else 1

    def halo_copy(field, part, where, src):
        if where == 1:
            device = (t + 1, r) if field == 0 else (t - 1, r)
            slot = (side_of(field), 1)
        else:
            device = (t, r - 1) if where == 0 else (t, r + 1)
            slot = (part, 2 - where)
        return pltpu.make_async_remote_copy(
            src_ref=src,
            dst_ref=exts[field].at[slot],
            send_sem=halo_send.at[field, part, where],
            recv_sem=halo_recv.at[field, slot[0], slot[1]],
            device_id=device,
            device_id_type=MESH,
        )

    def sends_time(field):
        return has_future if field == 0 else has_past

    def gets_time(field):
        return has_past if field == 0 else has_future

    row_side = {0: has_up, 2: has_down}

    def start_own(field, src):
        @pl.when(sends_time(field))
        def _():
            halo_copy(field, own_of(field), 1, src).start()

        for where in (0, 2):
            @pl.when(row_side[where])
            def _(where=where):
                halo_copy(field, own_of(field), where, src).start()

    def wait_slot(field, part, row):
        pltpu.make_async_remote_copy(
            src_ref=exts[field].at[part, row],
            dst_ref=exts[field].at[part, row],
            send_sem=halo_send.at[field, part, row],
            recv_sem=halo_recv.at[field, part, row],
            device_id=(t, r),
            device_id_type=MESH,
        ).wait_recv()

    def forward(field):
        side = side_of(field)

        @pl.when(gets_time(field))
        def _():
            wait_slot(field, side, 1)

        for where in (0, 2):
            @pl.when(jnp.logical_and(gets_time(field), row_side[where]))
            def _(where=where):
                halo_copy(field, side, where, exts[field].at[side, 1]).start()

    def wait_rows(field, part):
        for row in (0, 2):
            cond = row_side[row]
            if part == side_of(field):
                cond = jnp.logical_and(cond, gets_time(field))

            @pl.when(cond)
            def _(row=row):
                wait_slot(field, part, row)

    def finish_sends(field, src):
        side = side_of(field)

        @pl.when(sends_time(field))
        def _():
            halo_copy(field, own_of(field), 1, src).wait_send()

        for where in (0, 2):
            @pl.when(row_side[where])
            def _(where=where):
                halo_copy(field, own_of(field), where, src).wait_send()

            @pl.when(jnp.logical_and(gets_time(field), row_side[where]))
            def _(where=where):
                halo_copy(field, side, where, exts[field].at[side, 1]).wait_send()

    start_own(0, video)
    start_own(1, cotangent)

    zeros_block = jnp.zeros((2, C, W), BF16)
    for field in range(3):
        side = side_of(field)
        for row in range(3):
            cond = jnp.logical_not(gets_time(field))
            if row != 1:
                cond = jnp.logical_or(cond, jnp.logical_not(row_side[row]))

            @pl.when(cond)
            def _(field=field, side=side, row=row):
                exts[field][side, row] = zeros_block

            if row != 1:
                @pl.when(jnp.logical_not(row_side[row]))
                def _(field=field, row=row):
                    exts[field][own_of(field), row] = zeros_block

    def activate(part, row):
        for f in range(2):
            at = 2 * part + f
            value, _ = silu_parts(vext[part, row, f].astype(F32))
            acts[at, row] = value.astype(BF16)
            acts_t[row, at * W : (at + 1) * W, :] = jnp.transpose(value).astype(BF16)

    loads[0].wait()
    activate(1, 1)
    forward(0)
    forward(1)
    activate(0, 1)
    loads[2].wait()

    def conv_taps(row, tt, first):
        lhs = acts_t[row, tt * W : (tt + 2) * W, :]
        for q in range(3):
            tap = tt * 9 + row * 3 + q
            term = dot(lhs, k1[tap * C : (tap + 1) * C, :])
            if first:
                acc_t[q] = term
            else:
                acc_t[q] += term

    for tt in range(3):
        conv_taps(1, tt, tt == 0)
    wait_rows(0, 1)
    activate(1, 0)
    activate(1, 2)
    conv_taps(0, 2, False)
    conv_taps(2, 2, False)
    wait_rows(0, 0)
    activate(0, 0)
    activate(0, 2)
    for row in (0, 2):
        for tt in range(2):
            conv_taps(row, tt, False)
    for f in range(2):
        rows = slice(f * W, (f + 1) * W)
        out = sublane_shift(acc_t[0, rows], 1) + acc_t[1, rows] + sublane_shift(acc_t[2, rows], -1)
        x1[f] = jnp.transpose(out).astype(BF16)

    def field_pair(ext, tt, p):
        at = (2 - tt, 3 - tt)
        return jnp.concatenate([ext[a // 2, 2 - p, a % 2] for a in at], axis=1)

    def back_taps(ext, k_ref, tt, p, first):
        g = tt * 3 + p
        term = dot(k_ref[g * 576 : (g + 1) * 576, :], field_pair(ext, tt, p))
        if first:
            acc[...] = term
        else:
            acc[...] += term

    def back_sum(f):
        cols = slice(f * W, (f + 1) * W)
        return (
            lane_shift(acc[0:C, cols], -1)
            + acc[C : 2 * C, cols]
            + lane_shift(acc[2 * C : 3 * C, cols], 1)
        )

    loads[1].wait()
    loads[3].wait()
    wait_rows(1, 0)
    wait_rows(1, 1)
    for p in range(3):
        for tt in range(3):
            back_taps(cext, k2, tt, p, p == 0 and tt == 0)
    for f in range(2):
        _, slope = silu_parts(x1[f].astype(F32))
        gext[0, 1, f] = (back_sum(f) * slope).astype(BF16)
    start_own(2, gext.at[0, 1])

    zeros64 = jnp.zeros((64, 2 * W), BF16)

    def store_term(layer, start, term):
        n = term.shape[0]
        wa[layer, start : start + n, :] = term[:, :W].astype(BF16)
        if start < HALF:
            wb[layer, start : start + n, :] = term[:, W:].astype(BF16)
        else:
            wb[layer, start - HALF : start - HALF + n, :] += term[:, W:].astype(BF16)

    def widened(value, upper):
        lo, hi = value[:W], value[W:C]
        return jnp.concatenate([lo, zeros64, hi] if upper else [lo, hi, zeros64], axis=0)

    pair_blocks = []
    for h in range(2):
        for bx in range(2):
            for b in range(6):
                zi, kind = b // 3, b % 3
                z_to = 2 * h + zi + (4 if kind == 2 else 0)
                pair_blocks.append((h, bx, b, kind == 1, 4 * z_to + 2 * bx))

    def block_src(layer, packed, j):
        ref = wb if packed else wa
        return ref.at[layer, pl.ds(chunk_start(j), CHUNK), :]

    sibling = (t, r + 1 - 2 * c)

    def pair_copy(layer, h, bx, b, packed, j0):
        return pltpu.make_async_remote_copy(
            src_ref=block_src(layer, packed, j0 + 1 - c),
            dst_ref=pair_in.at[layer, h, bx, b],
            send_sem=pair_send.at[layer, h, bx, b],
            recv_sem=pair_recv.at[layer, h, bx, b],
            device_id=sibling,
            device_id_type=MESH,
        )

    def pair_start(layer):
        for block in pair_blocks:
            pair_copy(layer, *block).start()

    a2 = []
    for f in range(2):
        value, _ = silu_parts(x1[f].astype(F32))
        a2.append([lane_shift(value, 1), value, lane_shift(value, -1)])
    a2_taps = jnp.concatenate(
        [jnp.concatenate([a2[f][q].astype(BF16) for f in range(2)], axis=1) for q in range(3)], axis=0
    )
    acts2 = a2_taps
    for g in range(9):
        pair = field_pair(cext, g // 3, g % 3)
        if g < 4:
            store_term(1, 576 * g, dot_nt(acts2, widened(pair, False)))
        elif g == 4:
            store_term(1, 576 * g, dot_nt(acts2[:288], widened(pair, False)))
            store_term(1, HALF, dot_nt(acts2[288:], widened(pair, True)))
        else:
            store_term(1, 576 * g, dot_nt(acts2, widened(pair, True)))
    pair_start(1)

    g1 = [gext[0, 1, f].astype(F32) for f in range(2)]
    g1_taps = []
    for q in range(3):
        by = {0: -1, 2: 1}.get(q)
        cols = [g1[f] if by is None else lane_shift(g1[f], by) for f in range(2)]
        g1_taps.append(jnp.concatenate([v.astype(BF16) for v in cols], axis=1))
    g1_low = [widened(v, False) for v in g1_taps]
    g1_high = [widened(v, True) for v in g1_taps]
    for g in range(9):
        tt, p = g // 3, g % 3
        lhs = jnp.concatenate([acts[tt, p], acts[tt + 1, p]], axis=1)
        for q in range(3):
            start = 576 * g + C * q
            if start + C <= HALF:
                store_term(0, start, dot_nt(lhs, g1_low[q]))
            elif start >= HALF:
                store_term(0, start, dot_nt(lhs, g1_high[q]))
            else:
                store_term(0, start, dot_nt(lhs[:96], g1_low[q]))
                store_term(0, HALF, dot_nt(lhs[96:], g1_high[q]))
    pair_start(0)

    def dev(nxl, ny, nz, nxh):
        return (nxl * 4 + ny, nz * 4 + nxh * 2 + c)

    def s1_copies(layer):
        out = []
        for d in range(1, 4):
            ny = lax.rem(y + d, 4)
            out.append(
                pltpu.make_async_remote_copy(
                    src_ref=summed.at[layer, 0, :, :, pl.ds(pl.multiple_of(group_a(ny), 16), 48), :],
                    dst_ref=r1a.at[layer, d - 1],
                    send_sem=s1_send.at[layer, 0, d - 1],
                    recv_sem=s1_recv.at[layer, 0, d - 1],
                    device_id=dev(xl, ny, z, xh),
                    device_id_type=MESH,
                )
            )
            nx = lax.rem(x + d, 4)
            out.append(
                pltpu.make_async_remote_copy(
                    src_ref=summed.at[layer, 1, nx // 2, :, pl.ds(pl.multiple_of(80 * (nx % 2), 16), 96), :],
                    dst_ref=r1b.at[layer, d - 1],
                    send_sem=s1_send.at[layer, 1, d - 1],
                    recv_sem=s1_recv.at[layer, 1, d - 1],
                    device_id=dev(nx % 2, y, z, nx // 2),
                    device_id_type=MESH,
                )
            )
        return out

    def s2_copies(layer):
        out = []
        for d in range(1, 4):
            nx = lax.rem(x + d, 4)
            out.append(
                pltpu.make_async_remote_copy(
                    src_ref=ta.at[layer, nx // 2, :, pl.ds(pl.multiple_of(16 * (nx % 2), 16), 32), :],
                    dst_ref=r2a.at[layer, d - 1],
                    send_sem=s2_send.at[layer, 0, d - 1],
                    recv_sem=s2_recv.at[layer, 0, d - 1],
                    device_id=dev(nx % 2, y, z, nx // 2),
                    device_id_type=MESH,
                )
            )
            ny = lax.rem(y + d, 4)
            out.append(
                pltpu.make_async_remote_copy(
                    src_ref=tb.at[layer, :, pl.ds(pl.multiple_of(group_b(ny), 16), 32), :],
                    dst_ref=r2b.at[layer, d - 1],
                    send_sem=s2_send.at[layer, 1, d - 1],
                    recv_sem=s2_recv.at[layer, 1, d - 1],
                    device_id=dev(xl, ny, z, xh),
                    device_id_type=MESH,
                )
            )
        return out

    def z_block(nz):
        return (nz % 4) // 2, 3 * (nz % 2) + nz // 4

    def s3_copies(layer):
        out = []
        for d in range(1, 8):
            nz = lax.rem(z + d, 8)
            nh, nb = z_block(nz)
            out.append(
                pltpu.make_async_remote_copy(
                    src_ref=ub.at[layer, nh, pl.ds(nb, 2)],
                    dst_ref=r3.at[layer, d - 1],
                    send_sem=s3_send.at[layer, d - 1],
                    recv_sem=s3_recv.at[layer, d - 1],
                    device_id=dev(xl, y, nz, xh),
                    device_id_type=MESH,
                )
            )
        return out

    def s4_copies(layer):
        out = []
        for e in range(1, 8):
            out.append(
                pltpu.make_async_remote_copy(
                    src_ref=r4.at[layer, 0],
                    dst_ref=r4.at[layer, e],
                    send_sem=s4_send.at[layer, e - 1],
                    recv_sem=s4_recv.at[layer, e - 1],
                    device_id=(lax.rem(t + e, 8), r),
                    device_id_type=MESH,
                )
            )
        return out

    def wide(value):
        return value.astype(F32)

    def stage1(layer):
        for h, bx, b, packed, j0 in pair_blocks:
            pair_copy(layer, h, bx, b, packed, j0).wait()
            own = block_src(layer, packed, j0 + c)[...]
            summed[layer, h, bx, b] = (wide(own) + wide(pair_in[layer, h, bx, b])).astype(BF16)
        for copy in s1_copies(layer):
            copy.start()

    def stage2(layer):
        for copy in s1_copies(layer):
            copy.wait()
        for bx in range(2):
            for b in range(6):
                own = summed[layer, 0, bx, b, pl.ds(pl.multiple_of(group_a(y), 16), 48), :]
                ta[layer, bx, b] = (
                    wide(own) + wide(r1a[layer, 0, bx, b]) + wide(r1a[layer, 1, bx, b]) + wide(r1a[layer, 2, bx, b])
                ).astype(BF16)
        for b in range(6):
            own = summed[layer, 1, xh, b, pl.ds(pl.multiple_of(80 * xl, 16), 96), :]
            tb[layer, b] = (
                wide(own) + wide(r1b[layer, 0, b]) + wide(r1b[layer, 1, b]) + wide(r1b[layer, 2, b])
            ).astype(BF16)
        for copy in s2_copies(layer):
            copy.start()

    def stage3(layer):
        for copy in s2_copies(layer):
            copy.wait()
        for b in range(6):
            own = ta[layer, xh, b, pl.ds(pl.multiple_of(16 * xl, 16), 32), :]
            ub[layer, 0, b] = (
                wide(own) + wide(r2a[layer, 0, b]) + wide(r2a[layer, 1, b]) + wide(r2a[layer, 2, b])
            ).astype(BF16)
            own = tb[layer, b, pl.ds(pl.multiple_of(group_b(y), 16), 32), :]
            ub[layer, 1, b] = (
                wide(own) + wide(r2b[layer, 0, b]) + wide(r2b[layer, 1, b]) + wide(r2b[layer, 2, b])
            ).astype(BF16)
        for copy in s3_copies(layer):
            copy.start()

    my_half, my_block = z_block(z)
    scale = 1.0 / math.sqrt(TM * 2 * ROWS * W)

    def stage4(layer):
        for copy in s3_copies(layer):
            copy.wait()
        for k in range(2):
            total = wide(ub[layer, my_half, my_block + k])
            for d in range(7):
                total += wide(r3[layer, d, k])
            r4[layer, 0, k] = total.astype(BF16)
        for copy in s4_copies(layer):
            copy.start()

    def stage5(layer):
        for copy in s4_copies(layer):
            copy.wait()
        upper = z // 4
        for e in range(8):
            u = lax.rem(t + 8 - e, 8)
            uy, ux = u % 4, u // 4
            at_a = jnp.minimum(3 * uy, 8) + ux
            at_b = 5 * ux + uy + jnp.where(uy >= 2, 1, 0)
            start = pl.multiple_of(16 * jnp.where(my_half == 0, at_a, at_b), 16)
            main = wide(r4[layer, e, upper]) * scale
            rest = wide(r4[layer, e, 1 - upper]) * scale
            rest = jnp.where(upper == 0, rest, pltpu.roll(rest, 64, 1))
            final[pl.ds(start, 32), :W] = main
            final[pl.ds(start, 32), W:] = rest
        off = 4 * (z % 2) + 2 * xh + c
        for k in range(8):
            @pl.when(off == k)
            def _(k=k):
                k_grad[layer] = final[2 * k : 2 * k + 162, :C]

    stage1(1)
    forward(2)
    stage1(0)

    def back_rows(p):
        for tt in range(3):
            back_taps(gext, k1, tt, p, p == 1 and tt == 0)

    back_rows(1)
    wait_rows(2, 0)
    wait_rows(2, 1)
    back_rows(0)
    back_rows(2)
    for f in range(2):
        _, slope = silu_parts(vext[1, 1, f].astype(F32))
        in_grad[f, 0] = (back_sum(f) * slope).astype(BF16)

    stage2(1)
    stage2(0)
    stage3(1)
    stage3(0)
    stage4(1)
    stage4(0)
    stage5(1)
    stage5(0)

    finish_sends(0, video)
    finish_sends(1, cotangent)
    finish_sends(2, gext.at[0, 1])


def on_device(video_in, kernels, cotangent):
    dma = pltpu.SemaphoreType.DMA
    any_spec = pl.BlockSpec(memory_space=pl.ANY)
    vmem_spec = pl.BlockSpec(memory_space=pltpu.VMEM)
    return pl.pallas_call(
        kernel,
        out_shape=(
            jax.ShapeDtypeStruct((2, 1, C, W), BF16),
            jax.ShapeDtypeStruct((2, 162, C), F32),
        ),
        in_specs=[any_spec] * 3,
        out_specs=(vmem_spec, vmem_spec),
        scratch_shapes=[
            pltpu.VMEM((5184, C), BF16),
            pltpu.VMEM((5184, C), BF16),
            pltpu.VMEM((2, 3, 2, C, W), BF16),
            pltpu.VMEM((2, 3, 2, C, W), BF16),
            pltpu.VMEM((2, 3, 2, C, W), BF16),
            pltpu.VMEM((4, 3, C, W), BF16),
            pltpu.VMEM((3, 4 * W, C), BF16),
            pltpu.VMEM((3, 2 * W, C), F32),
            pltpu.VMEM((3 * C, 2 * W), F32),
            pltpu.VMEM((2, C, W), BF16),
            pltpu.VMEM((2, 5184, W), BF16),
            pltpu.VMEM((2, HALF, W), BF16),
            pltpu.VMEM((2, 2, 2, 6, CHUNK, W), BF16),
            pltpu.VMEM((2, 2, 2, 6, CHUNK, W), BF16),
            pltpu.VMEM((2, 3, 2, 6, 48, W), BF16),
            pltpu.VMEM((2, 3, 6, 96, W), BF16),
            pltpu.VMEM((2, 2, 6, 48, W), BF16),
            pltpu.VMEM((2, 6, 96, W), BF16),
            pltpu.VMEM((2, 3, 6, 32, W), BF16),
            pltpu.VMEM((2, 3, 6, 32, W), BF16),
            pltpu.VMEM((2, 2, 6, 32, W), BF16),
            pltpu.VMEM((2, 7, 2, 32, W), BF16),
            pltpu.VMEM((2, 8, 2, 32, W), BF16),
            pltpu.VMEM((CHUNK, 2 * W), F32),
            dma((4,)),
            dma((3, 2, 3)),
            dma((3, 2, 3)),
            dma((2, 2, 2, 6)),
            dma((2, 2, 2, 6)),
            dma((2, 2, 3)),
            dma((2, 2, 3)),
            dma((2, 2, 3)),
            dma((2, 2, 3)),
            dma((2, 7)),
            dma((2, 7)),
            dma((2, 7)),
            dma((2, 7)),
        ],
        compiler_params=pltpu.CompilerParams(
            collective_id=0, has_side_effects=True, vmem_limit_bytes=56 * 2**20
        ),
        cost_estimate=pl.CostEstimate(flops=2600000000, bytes_accessed=6000000, transcendentals=500000),
    )(video_in.reshape(2, C, W), kernels, cotangent.reshape(2, C, W))


def solution(mesh):
    return jax.shard_map(
        on_device,
        mesh=mesh,
        in_specs=(P("tm", "rows", None, None), P(), P("tm", "rows", None, None)),
        out_specs=(P("tm", "rows", None, None), P(None, "rows", None)),
        check_vma=False,
    )
```

time: 492 us -> 75 us (0.15)
  waiting for transfers between devices: 355 us -> 0 us
  Pallas kernels: 0 us -> 62.3 us
  local copies, waits for them, and re-layouts: 59.7 us -> 10.7 us
  starting transfers between devices: 41.6 us -> 0 us
  between operations: 15.4 us -> 0.64 us
  other arithmetic: 11.3 us -> 0 us
  matrix products: 7.37 us -> 0 us
    unnamed x3 -> x0, waiting for transfers between devices: 271 us -> none
    psum x1 -> x0, waiting for transfers between devices: 76 us -> none  [on_device(): summed = lax.psum(share, 'tm')]
    pallas_call x0 -> x1, Pallas kernels: none -> 62.3 us  [on_device(): pl.pallas_call(kernel, out_shape=(jax.ShapeDtypeStruct((2, 1, C, W), BF16...]
    ppermute x12 -> x0, starting transfers between devices: 41.5 us -> none  [the longest x4 23.5 us: padded(): before = lax.ppermute(last, axis, up)]
    unnamed x114 -> x2, local copies, waits for them, and re-layouts: 27.6 us -> 8.85 us
    another operation x1 -> x0, local copies, waits for them, and re-layouts: 16.1 us -> none  [on_device(): jnp.stack(local_terms)]
    ppermute x12 -> x0, waiting for transfers between devices: 8.52 us -> none  [the longest x4 8.5 us: from_behind(): lax.ppermute(value, axis, [(source, source + steps) for source in range(i...]
    slice x2 -> x0, local copies, waits for them, and re-layouts: 8.25 us -> none  [on_device(): kernels[layer_id].reshape(27, channel, channel).transpose(1, 0, 2)]
  transfers between devices with their start and end apart: 14 -> 0, of which waited for: 4 -> 0; matrix products, arithmetic and copies ran while one was open for 10% -> 0% of each run, Pallas kernels for 0% -> 0%
where the time goes in v1:
time: 75 us; the launch traced here: 73.7 us
  Pallas kernels  62.3 us (83%)
  local copies, waits for them, and re-layouts  10.7 us (14%)
    pallas_call x1, Pallas kernels, on_device(): pl.pallas_call(kernel, out_shape=(jax.ShapeDtypeStruct((2, 1, C, W), BF16...  62.3 us
    unnamed x2, local copies, waits for them, and re-layouts  8.85 us
    pallas_call x1, local copies, waits for them, and re-layouts, on_device(): pl.pallas_call(kernel, out_shape=(jax.ShapeDtypeStruct((2, 1, C, W), BF16...  1.88 us

profile of v1, /device:TPU:2, one launch (start us, length us, event | category | flops | bytes accessed | tf_op | source)
XLA Modules:
  0.0 73.7 jit_solution(14290719945210114155)
XLA Ops:
  0.6 7.3 %copy.5.kernels = bf16[2,5184,192]{2,1,0:T(8,128)(2,1)} copy(bf16[2,5184,192]{1,2,0:T(8,128)(2,1)} %param.4) | data formatting | bytes 7962624 | tf_op args[1]
  7.9 62.3 %shard_map.50 = (bf16[2,1,192,128]{3,2,1,0:T(8,128)(2,1)}, f32[2,162,192]{2,1,0:T(8,128)}) custom-call(bf16[2,192,128]{2,1,0:T(8,128)(2,1)} %bitcast.2, bf16[2,5184,192]{2,1,0:T(8,128)(2,1)} %copy.5.kernels, bf16[2,192,128]{2,1,0:T(8,128)(2,1)} %bitcast.3), custom_call_target="tpu_custom_call" | custom-call | flops 2600000000 | bytes 6000000 | tf_op jit(solution)/shard_map/pallas_call | solution.py:578
  70.3 1.9 %copy.6 = f32[2,162,192]{2,0,1:T(2,128)} copy(f32[2,162,192]{2,1,0:T(8,128)} %get-tuple-element.3) | data formatting | bytes 497664 | tf_op jit(solution)/shard_map/pallas_call | solution.py:578
  72.1 1.5 %copy.8 = bf16[2,1,192,128]{3,2,1,0:T(8,128)(2,1)} copy(bf16[2,1,192,128]{3,2,1,0:T(8,128)(2,1)} %get-tuple-element.6) | data formatting | bytes 196608

commit v2 on v1

--- a/solution.py
+++ b/solution.py
@@ -33,13 +33,6 @@
     return jnp.where(col == edge, 0.0, rolled)
 
 
-def sublane_shift(value, by):
-    rolled = pltpu.roll(value, by % W, 0)
-    row = lax.broadcasted_iota(jnp.int32, value.shape, 0)
-    edge = 0 if by == 1 else W - 1
-    return jnp.where(row == edge, 0.0, rolled)
-
-
 def silu_parts(value):
     sigma = jax.nn.sigmoid(value)
     return value * sigma, sigma * (1.0 + value * (1.0 - sigma))
@@ -59,7 +52,7 @@
 
 def kernel(
     video, kernels, cotangent, in_grad, k_grad,
-    k1, k2, vext, cext, gext, acts, acts_t, acc_t, acc, x1, wa, wb, pair_in, summed,
+    k1t, k2t, k1, k2, vext, cext, gext, stack, acts2, acc, x1, wa, wb, pair_in, summed,
     r1a, r1b, ta, tb, r2a, r2b, ub, r3, r4, final,
     load_sem, halo_send, halo_recv, pair_send, pair_recv,
     s1_send, s1_recv, s2_send, s2_recv, s3_send, s3_recv, s4_send, s4_recv,
@@ -75,8 +68,8 @@
     loads = [
         pltpu.make_async_copy(video, vext.at[1, 1], load_sem.at[0]),
         pltpu.make_async_copy(cotangent, cext.at[0, 1], load_sem.at[1]),
-        pltpu.make_async_copy(kernels.at[0], k1, load_sem.at[2]),
-        pltpu.make_async_copy(kernels.at[1], k2, load_sem.at[3]),
+        pltpu.make_async_copy(kernels.at[0], k1t, load_sem.at[2]),
+        pltpu.make_async_copy(kernels.at[1], k2t, load_sem.at[3]),
     ]
     for load in loads:
         load.start()
@@ -217,89 +210,48 @@
         for f in range(2):
             at = 2 * part + f
             value, _ = silu_parts(vext[part, row, f].astype(F32))
-            acts[at, row] = value.astype(BF16)
-            acts_t[row, at * W : (at + 1) * W, :] = jnp.transpose(value).astype(BF16)
+            shifted = (lane_shift(value, 1), value, lane_shift(value, -1))
+            for q in range(3):
+                block = shifted[q].astype(BF16)
+                for to in range(2):
+                    tt = at - to
+                    if 0 <= tt <= 2:
+                        start = (tt * 9 + row * 3 + q) * C
+                        stack[start : start + C, to * W : (to + 1) * W] = block
+
+    def turn(src, dst):
+        for start in range(0, 5184, W):
+            n = min(W, 5184 - start)
+            dst[start : start + n, :] = jnp.transpose(src[:, start : start + n])
 
     loads[0].wait()
     activate(1, 1)
+    loads[3].wait()
     forward(0)
+    turn(k2t, k2)
     forward(1)
     activate(0, 1)
-    loads[2].wait()
-
-    def conv_taps(row, tt, first):
-        lhs = acts_t[row, tt * W : (tt + 2) * W, :]
-        for q in range(3):
-            tap = tt * 9 + row * 3 + q
-            term = dot(lhs, k1[tap * C : (tap + 1) * C, :])
-            if first:
-                acc_t[q] = term
-            else:
-                acc_t[q] += term
-
-    for tt in range(3):
-        conv_taps(1, tt, tt == 0)
     wait_rows(0, 1)
     activate(1, 0)
     activate(1, 2)
-    conv_taps(0, 2, False)
-    conv_taps(2, 2, False)
+    loads[2].wait()
+    late = dot(k1t[:, 3456:], stack[3456:, :])
     wait_rows(0, 0)
     activate(0, 0)
     activate(0, 2)
-    for row in (0, 2):
-        for tt in range(2):
-            conv_taps(row, tt, False)
+    out = late + dot(k1t[:, :3456], stack[:3456, :])
     for f in range(2):
-        rows = slice(f * W, (f + 1) * W)
-        out = sublane_shift(acc_t[0, rows], 1) + acc_t[1, rows] + sublane_shift(acc_t[2, rows], -1)
-        x1[f] = jnp.transpose(out).astype(BF16)
+        x1[f] = out[:, f * W : (f + 1) * W].astype(BF16)
+
+    zeros64 = jnp.zeros((64, 2 * W), BF16)
+
+    def widened(value, upper):
+        lo, hi = value[:W], value[W:C]
+        return jnp.concatenate([lo, zeros64, hi] if upper else [lo, hi, zeros64], axis=0)
 
     def field_pair(ext, tt, p):
         at = (2 - tt, 3 - tt)
         return jnp.concatenate([ext[a // 2, 2 - p, a % 2] for a in at], axis=1)
-
-    def back_taps(ext, k_ref, tt, p, first):
-        g = tt * 3 + p
-        term = dot(k_ref[g * 576 : (g + 1) * 576, :], field_pair(ext, tt, p))
-        if first:
-            acc[...] = term
-        else:
-            acc[...] += term
-
-    def back_sum(f):
-        cols = slice(f * W, (f + 1) * W)
-        return (
-            lane_shift(acc[0:C, cols], -1)
-            + acc[C : 2 * C, cols]
-            + lane_shift(acc[2 * C : 3 * C, cols], 1)
-        )
-
-    loads[1].wait()
-    loads[3].wait()
-    wait_rows(1, 0)
-    wait_rows(1, 1)
-    for p in range(3):
-        for tt in range(3):
-            back_taps(cext, k2, tt, p, p == 0 and tt == 0)
-    for f in range(2):
-        _, slope = silu_parts(x1[f].astype(F32))
-        gext[0, 1, f] = (back_sum(f) * slope).astype(BF16)
-    start_own(2, gext.at[0, 1])
-
-    zeros64 = jnp.zeros((64, 2 * W), BF16)
-
-    def store_term(layer, start, term):
-        n = term.shape[0]
-        wa[layer, start : start + n, :] = term[:, :W].astype(BF16)
-        if start < HALF:
-            wb[layer, start : start + n, :] = term[:, W:].astype(BF16)
-        else:
-            wb[layer, start - HALF : start - HALF + n, :] += term[:, W:].astype(BF16)
-
-    def widened(value, upper):
-        lo, hi = value[:W], value[W:C]
-        return jnp.concatenate([lo, zeros64, hi] if upper else [lo, hi, zeros64], axis=0)
 
     pair_blocks = []
     for h in range(2):
@@ -308,6 +260,10 @@
                 zi, kind = b // 3, b % 3
                 z_to = 2 * h + zi + (4 if kind == 2 else 0)
                 pair_blocks.append((h, bx, b, kind == 1, 4 * z_to + 2 * bx))
+
+    def ready_at(block):
+        j = block[4] % 16 + 1
+        return -(-(16 * ((81 * j) // 8) + CHUNK) // 288) - 1
 
     def block_src(layer, packed, j):
         ref = wb if packed else wa
@@ -325,50 +281,60 @@
             device_id_type=MESH,
         )
 
-    def pair_start(layer):
-        for block in pair_blocks:
-            pair_copy(layer, *block).start()
-
-    a2 = []
+    def kernel_terms(layer, term):
+        for k in range(9):
+            at = 288 * k
+            low, high = term(k, False), term(k + 9, True)
+            wa[layer, at : at + 288, :] = low[:, :W].astype(BF16)
+            wa[layer, HALF + at : HALF + at + 288, :] = high[:, :W].astype(BF16)
+            wb[layer, at : at + 288, :] = (low[:, W:] + high[:, W:]).astype(BF16)
+            for block in pair_blocks:
+                if ready_at(block) == k:
+                    pair_copy(layer, *block).start()
+
+    def back_terms(ext, k_ref, p, first):
+        for tt in range(3):
+            g = tt * 3 + p
+            term = dot(k_ref[g * 576 : (g + 1) * 576, :], field_pair(ext, tt, p))
+            if first and tt == 0:
+                acc[...] = term
+            else:
+                acc[...] += term
+
+    def back_sum(f):
+        cols = slice(f * W, (f + 1) * W)
+        return (
+            lane_shift(acc[0:C, cols], -1)
+            + acc[C : 2 * C, cols]
+            + lane_shift(acc[2 * C : 3 * C, cols], 1)
+        )
+
     for f in range(2):
         value, _ = silu_parts(x1[f].astype(F32))
-        a2.append([lane_shift(value, 1), value, lane_shift(value, -1)])
-    a2_taps = jnp.concatenate(
-        [jnp.concatenate([a2[f][q].astype(BF16) for f in range(2)], axis=1) for q in range(3)], axis=0
-    )
-    acts2 = a2_taps
-    for g in range(9):
-        pair = field_pair(cext, g // 3, g % 3)
-        if g < 4:
-            store_term(1, 576 * g, dot_nt(acts2, widened(pair, False)))
-        elif g == 4:
-            store_term(1, 576 * g, dot_nt(acts2[:288], widened(pair, False)))
-            store_term(1, HALF, dot_nt(acts2[288:], widened(pair, True)))
-        else:
-            store_term(1, 576 * g, dot_nt(acts2, widened(pair, True)))
-    pair_start(1)
-
-    g1 = [gext[0, 1, f].astype(F32) for f in range(2)]
-    g1_taps = []
-    for q in range(3):
-        by = {0: -1, 2: 1}.get(q)
-        cols = [g1[f] if by is None else lane_shift(g1[f], by) for f in range(2)]
-        g1_taps.append(jnp.concatenate([v.astype(BF16) for v in cols], axis=1))
-    g1_low = [widened(v, False) for v in g1_taps]
-    g1_high = [widened(v, True) for v in g1_taps]
-    for g in range(9):
-        tt, p = g // 3, g % 3
-        lhs = jnp.concatenate([acts[tt, p], acts[tt + 1, p]], axis=1)
+        shifted = (lane_shift(value, 1), value, lane_shift(value, -1))
         for q in range(3):
-            start = 576 * g + C * q
-            if start + C <= HALF:
-                store_term(0, start, dot_nt(lhs, g1_low[q]))
-            elif start >= HALF:
-                store_term(0, start, dot_nt(lhs, g1_high[q]))
-            else:
-                store_term(0, start, dot_nt(lhs[:96], g1_low[q]))
-                store_term(0, HALF, dot_nt(lhs[96:], g1_high[q]))
-    pair_start(0)
+            acts2[q * C : (q + 1) * C, f * W : (f + 1) * W] = shifted[q].astype(BF16)
+    loads[1].wait()
+    wait_rows(1, 0)
+    wait_rows(1, 1)
+
+    def second_term(hg, upper):
+        g, part = hg // 2, hg % 2
+        pair = widened(field_pair(cext, g // 3, g % 3), upper)
+        return dot_nt(acts2[288 * part : 288 * part + 288, :], pair)
+
+    kernel_terms(1, second_term)
+
+    for p in range(3):
+        back_terms(cext, k2, p, p == 0)
+    for f in range(2):
+        _, slope = silu_parts(x1[f].astype(F32))
+        gext[0, 1, f] = (back_sum(f) * slope).astype(BF16)
+    start_own(2, gext.at[0, 1])
+
+    def first_term(hg, upper):
+        pair = jnp.concatenate([gext[0, 1, 0], gext[0, 1, 1]], axis=1)
+        return dot_nt(stack[288 * hg : 288 * hg + 288, :], widened(pair, upper))
 
     def dev(nxl, ny, nz, nxh):
         return (nxl * 4 + ny, nz * 4 + nxh * 2 + c)
@@ -541,18 +507,15 @@
                 k_grad[layer] = final[2 * k : 2 * k + 162, :C]
 
     stage1(1)
+    kernel_terms(0, first_term)
     forward(2)
     stage1(0)
-
-    def back_rows(p):
-        for tt in range(3):
-            back_taps(gext, k1, tt, p, p == 1 and tt == 0)
-
-    back_rows(1)
+    turn(k1t, k1)
+    back_terms(gext, k1, 1, True)
     wait_rows(2, 0)
     wait_rows(2, 1)
-    back_rows(0)
-    back_rows(2)
+    back_terms(gext, k1, 0, False)
+    back_terms(gext, k1, 2, False)
     for f in range(2):
         _, slope = silu_parts(vext[1, 1, f].astype(F32))
         in_grad[f, 0] = (back_sum(f) * slope).astype(BF16)
@@ -584,14 +547,15 @@
         in_specs=[any_spec] * 3,
         out_specs=(vmem_spec, vmem_spec),
         scratch_shapes=[
+            pltpu.VMEM((C, 5184), BF16),
+            pltpu.VMEM((C, 5184), BF16),
             pltpu.VMEM((5184, C), BF16),
             pltpu.VMEM((5184, C), BF16),
             pltpu.VMEM((2, 3, 2, C, W), BF16),
             pltpu.VMEM((2, 3, 2, C, W), BF16),
             pltpu.VMEM((2, 3, 2, C, W), BF16),
-            pltpu.VMEM((4, 3, C, W), BF16),
-            pltpu.VMEM((3, 4 * W, C), BF16),
-            pltpu.VMEM((3, 2 * W, C), F32),
+            pltpu.VMEM((5184, 2 * W), BF16),
+            pltpu.VMEM((3 * C, 2 * W), BF16),
             pltpu.VMEM((3 * C, 2 * W), F32),
             pltpu.VMEM((2, C, W), BF16),
             pltpu.VMEM((2, 5184, W), BF16),
@@ -626,7 +590,7 @@
             collective_id=0, has_side_effects=True, vmem_limit_bytes=56 * 2**20
         ),
         cost_estimate=pl.CostEstimate(flops=2600000000, bytes_accessed=6000000, transcendentals=500000),
-    )(video_in.reshape(2, C, W), kernels, cotangent.reshape(2, C, W))
+    )(video_in.reshape(2, C, W), jnp.swapaxes(kernels, 1, 2), cotangent.reshape(2, C, W))
 
 
 def solution(mesh):

time: 75 us -> 68.8 us (0.917)
  local copies, waits for them, and re-layouts: 10.7 us -> 3.41 us
  Pallas kernels: 62.3 us -> 64.1 us
    unnamed x2 -> x1, local copies, waits for them, and re-layouts: 8.85 us -> 1.54 us
    pallas_call x1, Pallas kernels: 62.3 us -> 64.1 us  [on_device(): pl.pallas_call(kernel, out_shape=(jax.ShapeDtypeStruct((2, 1, C, W), BF16...]
where the time goes in v2:
time: 68.8 us; the launch traced here: 68.1 us
  Pallas kernels  64.1 us (93%)
  local copies, waits for them, and re-layouts  3.41 us (5%)
    pallas_call x1, Pallas kernels, on_device(): pl.pallas_call(kernel, out_shape=(jax.ShapeDtypeStruct((2, 1, C, W), BF16...  64.1 us
    pallas_call x1, local copies, waits for them, and re-layouts, on_device(): pl.pallas_call(kernel, out_shape=(jax.ShapeDtypeStruct((2, 1, C, W), BF16...  1.88 us
    unnamed x1, local copies, waits for them, and re-layouts  1.54 us

profile of v2, /device:TPU:2, one launch (start us, length us, event | category | flops | bytes accessed | tf_op | source)
XLA Modules:
  0.0 68.1 jit_solution(12269608216032393003)
XLA Ops:
  0.6 64.1 %shard_map.50 = (bf16[2,1,192,128]{3,2,1,0:T(8,128)(2,1)}, f32[2,162,192]{2,1,0:T(8,128)}) custom-call(bf16[2,192,128]{2,1,0:T(8,128)(2,1)} %bitcast.4, bf16[2,192,5184]{2,1,0:T(8,128)(2,1)} %bitcast.3, bf16[2,192,128]{2,1,0:T(8,128)(2,1)} %bitcast.5), custom_call_target="tpu_custom_call" | custom-call | flops 2600000000 | bytes 6000000 | tf_op jit(solution)/shard_map/pallas_call | solution.py:541
  64.7 1.9 %copy.5 = f32[2,162,192]{2,0,1:T(2,128)} copy(f32[2,162,192]{2,1,0:T(8,128)} %get-tuple-element.3) | data formatting | bytes 497664 | tf_op jit(solution)/shard_map/pallas_call | solution.py:541
  66.6 1.5 %copy.7 = bf16[2,1,192,128]{3,2,1,0:T(8,128)(2,1)} copy(bf16[2,1,192,128]{3,2,1,0:T(8,128)(2,1)} %get-tuple-element.6) | data formatting | bytes 196608

commit v3 on v2

v3 whole, which is shorter than its diff:
```python
import math

import jax
import jax.numpy as jnp
from jax import lax
from jax.experimental import pallas as pl
from jax.experimental.pallas import tpu as pltpu
from jax.sharding import PartitionSpec as P

MESH = pl.DeviceIdType.MESH
F32 = jnp.float32
BF16 = jnp.bfloat16
C = 192
W = 128
TM = 8
ROWS = 32
HALF = 2592
CHUNK = 176


def dot(a, b):
    return lax.dot_general(a, b, (((1,), (0,)), ((), ())), preferred_element_type=F32)


def dot_nt(a, b):
    return lax.dot_general(a, b, (((1,), (1,)), ((), ())), preferred_element_type=F32)


def lane_shift(value, by):
    rolled = pltpu.roll(value, by % W, 1)
    col = lax.broadcasted_iota(jnp.int32, value.shape, 1)
    edge = 0 if by == 1 else W - 1
    return jnp.where(col == edge, 0.0, rolled)


def silu_parts(value):
    sigma = jax.nn.sigmoid(value)
    return value * sigma, sigma * (1.0 + value * (1.0 - sigma))


def chunk_start(j):
    return pl.multiple_of(16 * ((81 * j) // 8), 16)


def kernel(
    video, kernels, cotangent, in_grad, k_grad,
    k1t, k2t, k1, k2, vext, cext, gext, stack, acts2, acc, x1, wa, wb, pair_in, summed,
    r1a, r1b, ta, tb, r2a, r2b, ub, r3, rz1, tz, rz2, tc, rp, r4, final,
    load_sem, halo_send, halo_recv, pair_send, pair_recv,
    s1_send, s1_recv, s2_send, s2_recv, s3_send, s3_recv, z1_send, z1_recv, z2_send, z2_recv,
    p_send, p_recv, s4_send, s4_recv,
):
    t = lax.axis_index("tm")
    r = lax.axis_index("rows")
    xl, y = t // 4, t % 4
    z, xh, c = r // 4, (r // 2) % 2, r % 2
    x = 2 * xh + xl
    has_far = jnp.logical_and(r > 0, r < ROWS - 1)
    far_row, sibling_row = r - 1 + 2 * c, r + 1 - 2 * c
    far_slot, sibling_slot = 2 * c, 2 - 2 * c
    has_past, has_future = t > 0, t < TM - 1

    loads = [
        pltpu.make_async_copy(video, vext.at[1, 1], load_sem.at[0]),
        pltpu.make_async_copy(cotangent, cext.at[0, 1], load_sem.at[1]),
        pltpu.make_async_copy(kernels.at[0], k1t, load_sem.at[2]),
        pltpu.make_async_copy(kernels.at[1], k2t, load_sem.at[3]),
    ]
    for load in loads:
        load.start()

    barrier = pltpu.get_barrier_semaphore()

    def greet(device):
        pl.semaphore_signal(barrier, inc=1, device_id=device, device_id_type=MESH)

    for e in range(1, 8):
        greet((lax.rem(t + e, 8), r))
        greet((t, lax.rem(z + e, 8) * 4 + xh * 2 + c))
    for e in range(8):
        greet((lax.rem(t + e, 8), z * 4 + (1 - xh) * 2 + c))
    greet((t, sibling_row))

    @pl.when(has_far)
    def _():
        greet((t, far_row))

    pl.semaphore_wait(barrier, 23 + jnp.where(has_far, 1, 0))

    exts = (vext, cext, gext)

    def own_of(field):
        return 1 if field == 0 else 0

    def side_of(field):
        return 0 if field == 0 else 1

    def sends_time(field):
        return has_future if field == 0 else has_past

    def gets_time(field):
        return has_past if field == 0 else has_future

    def halo_copy(field, which, src=None):
        own, side, ext = own_of(field), side_of(field), exts[field]
        time_device = (t + 1, r) if field == 0 else (t - 1, r)
        if which == 0:
            device, part, row = (t, far_row), own, 2 - 2 * c
        elif which == 1:
            device, part, row = (t, sibling_row), own, 2 * c
        elif which == 2:
            device, part, row = time_device, side, 1
        elif which == 3:
            src, device, part, row = ext.at[own, far_slot], time_device, side, far_slot
        else:
            src, device, part, row = ext.at[side, 1], (t, sibling_row), side, 2 * c
        return pltpu.make_async_remote_copy(
            src_ref=src,
            dst_ref=ext.at[part, row],
            send_sem=halo_send.at[field, which],
            recv_sem=halo_recv.at[field, part, row],
            device_id=device,
            device_id_type=MESH,
        )

    def sends(field, which):
        return (
            has_far,
            None,
            sends_time(field),
            jnp.logical_and(has_far, sends_time(field)),
            gets_time(field),
        )[which]

    def when(cond, act):
        if cond is None:
            act()
        else:
            pl.when(cond)(act)

    def start_own(field, src):
        for which in (0, 2, 1):
            when(sends(field, which), lambda which=which: halo_copy(field, which, src).start())

    def wait_slot(field, part, row):
        pltpu.make_async_remote_copy(
            src_ref=exts[field].at[part, row],
            dst_ref=exts[field].at[part, row],
            send_sem=halo_send.at[field, 0],
            recv_sem=halo_recv.at[field, part, row],
            device_id=(t, sibling_row),
            device_id_type=MESH,
        ).wait_recv()

    def forward(field):
        own, side = own_of(field), side_of(field)
        when(has_far, lambda: wait_slot(field, own, far_slot))
        when(sends(field, 3), lambda: halo_copy(field, 3).start())
        when(gets_time(field), lambda: wait_slot(field, side, 1))
        when(sends(field, 4), lambda: halo_copy(field, 4).start())

    def wait_corners(field):
        side = side_of(field)
        when(jnp.logical_and(has_far, gets_time(field)), lambda: wait_slot(field, side, far_slot))
        when(gets_time(field), lambda: wait_slot(field, side, sibling_slot))

    def finish_sends(field, src):
        for which in range(5):
            when(sends(field, which), lambda which=which: halo_copy(field, which, src).wait_send())

    start_own(0, video)
    start_own(1, cotangent)

    zeros_block = jnp.zeros((2, C, W), BF16)

    def clear(field, part, row):
        exts[field][part, row] = zeros_block

    for field in range(3):
        own, side = own_of(field), side_of(field)
        no_time = jnp.logical_not(gets_time(field))
        no_far = jnp.logical_not(has_far)
        when(no_far, lambda: clear(field, own, far_slot))
        when(no_time, lambda: clear(field, side, 1))
        when(no_time, lambda: clear(field, side, sibling_slot))
        when(jnp.logical_or(no_time, no_far), lambda: clear(field, side, far_slot))

    def activate(part, row):
        for f in range(2):
            at = 2 * part + f
            value, _ = silu_parts(vext[part, row, f].astype(F32))
            shifted = (lane_shift(value, 1), value, lane_shift(value, -1))
            for q in range(3):
                block = shifted[q].astype(BF16)
                for to in range(2):
                    tt = at - to
                    if 0 <= tt <= 2:
                        start = (tt * 9 + row * 3 + q) * C
                        stack[start : start + C, to * W : (to + 1) * W] = block

    def turn(src, dst):
        for start in range(0, 5184, W):
            n = min(W, 5184 - start)
            dst[start : start + n, :] = jnp.transpose(src[:, start : start + n])

    loads[0].wait()
    activate(1, 1)
    loads[3].wait()
    turn(k2t, k2)
    loads[2].wait()
    turn(k1t, k1)
    forward(0)
    activate(0, 1)
    wait_slot(0, 1, sibling_slot)
    activate(1, 0)
    activate(1, 2)
    forward(1)
    late = dot(k1t[:, 3456:], stack[3456:, :])
    wait_corners(0)
    activate(0, 0)
    activate(0, 2)
    out = late + dot(k1t[:, :3456], stack[:3456, :])
    for f in range(2):
        x1[f] = out[:, f * W : (f + 1) * W].astype(BF16)

    zeros64 = jnp.zeros((64, 2 * W), BF16)

    def widened(value, upper):
        lo, hi = value[:W], value[W:C]
        return jnp.concatenate([lo, zeros64, hi] if upper else [lo, hi, zeros64], axis=0)

    def field_pair(ext, tt, p):
        at = (2 - tt, 3 - tt)
        return jnp.concatenate([ext[a // 2, 2 - p, a % 2] for a in at], axis=1)

    pair_blocks = []
    for h in range(2):
        for bx in range(2):
            for b in range(6):
                zi, kind = b // 3, b % 3
                z_to = 2 * h + zi + (4 if kind == 2 else 0)
                pair_blocks.append((h, bx, b, kind == 1, 4 * z_to + 2 * bx))

    def ready_at(block):
        j = block[4] % 16 + 1
        return -(-(16 * ((81 * j) // 8) + CHUNK) // 288) - 1

    def block_src(layer, packed, j):
        ref = wb if packed else wa
        return ref.at[layer, pl.ds(chunk_start(j), CHUNK), :]

    sibling = (t, sibling_row)

    def pair_copy(layer, h, bx, b, packed, j0):
        return pltpu.make_async_remote_copy(
            src_ref=block_src(layer, packed, j0 + 1 - c),
            dst_ref=pair_in.at[layer, h, bx, b],
            send_sem=pair_send.at[layer, h, bx, b],
            recv_sem=pair_recv.at[layer, h, bx, b],
            device_id=sibling,
            device_id_type=MESH,
        )

    def kernel_terms(layer, term):
        for k in range(9):
            at = 288 * k
            low, high = term(k, False), term(k + 9, True)
            wa[layer, at : at + 288, :] = low[:, :W].astype(BF16)
            wa[layer, HALF + at : HALF + at + 288, :] = high[:, :W].astype(BF16)
            wb[layer, at : at + 288, :] = (low[:, W:] + high[:, W:]).astype(BF16)
            for block in pair_blocks:
                if ready_at(block) == k:
                    pair_copy(layer, *block).start()

    def back_terms(ext, k_ref, p, first):
        for tt in range(3):
            g = tt * 3 + p
            term = dot(k_ref[g * 576 : (g + 1) * 576, :], field_pair(ext, tt, p))
            if first and tt == 0:
                acc[...] = term
            else:
                acc[...] += term

    def back_sum(f):
        cols = slice(f * W, (f + 1) * W)
        return (
            lane_shift(acc[0:C, cols], -1)
            + acc[C : 2 * C, cols]
            + lane_shift(acc[2 * C : 3 * C, cols], 1)
        )

    for f in range(2):
        value, _ = silu_parts(x1[f].astype(F32))
        shifted = (lane_shift(value, 1), value, lane_shift(value, -1))
        for q in range(3):
            acts2[q * C : (q + 1) * C, f * W : (f + 1) * W] = shifted[q].astype(BF16)
    loads[1].wait()
    wait_slot(1, 0, sibling_slot)
    wait_corners(1)

    def second_term(hg, upper):
        g, part = hg // 2, hg % 2
        pair = widened(field_pair(cext, g // 3, g % 3), upper)
        return dot_nt(acts2[288 * part : 288 * part + 288, :], pair)

    kernel_terms(1, second_term)

    for p in range(3):
        back_terms(cext, k2, p, p == 0)
    for f in range(2):
        _, slope = silu_parts(x1[f].astype(F32))
        gext[0, 1, f] = (back_sum(f) * slope).astype(BF16)
    start_own(2, gext.at[0, 1])

    def first_term(hg, upper):
        pair = jnp.concatenate([gext[0, 1, 0], gext[0, 1, 1]], axis=1)
        return dot_nt(stack[288 * hg : 288 * hg + 288, :], widened(pair, upper))

    def dev(nxl, ny, nz, nxh):
        return (nxl * 4 + ny, nz * 4 + nxh * 2 + c)

    def remote(src, dst, sems, at, device):
        return pltpu.make_async_remote_copy(
            src_ref=src,
            dst_ref=dst,
            send_sem=sems[0].at[at],
            recv_sem=sems[1].at[at],
            device_id=device,
            device_id_type=MESH,
        )

    def rows_at(start, n):
        return pl.ds(pl.multiple_of(start, 16), n)

    def z_block(nz):
        return (nz % 4) // 2, 3 * (nz % 2) + nz // 4

    def s1_copies(layer):
        out = []
        for d in range(1, 4):
            ny, nx = lax.rem(y + d, 4), lax.rem(x + d, 4)
            src = summed.at[layer, 0, :, :, rows_at(32 * ny, 32), :]
            out.append(remote(src, r1a.at[layer, d - 1], (s1_send, s1_recv), (layer, 0, d - 1), dev(xl, ny, z, xh)))
            src = summed.at[layer, 1, nx // 2, :, rows_at(64 * (nx % 2), 64), :]
            out.append(
                remote(src, r1b.at[layer, d - 1], (s1_send, s1_recv), (layer, 1, d - 1), dev(nx % 2, y, z, nx // 2))
            )
        return out

    def s2_copies(layer):
        out = []
        for d in range(1, 4):
            ny, nx = lax.rem(y + d, 4), lax.rem(x + d, 4)
            src = ta.at[layer, nx // 2, :, rows_at(16 * (nx % 2), 16), :]
            out.append(
                remote(src, r2a.at[layer, d - 1], (s2_send, s2_recv), (layer, 0, d - 1), dev(nx % 2, y, z, nx // 2))
            )
            src = tb.at[layer, :, rows_at(16 * ny, 16), :]
            out.append(remote(src, r2b.at[layer, d - 1], (s2_send, s2_recv), (layer, 1, d - 1), dev(xl, ny, z, xh)))
        return out

    def s3_copies(layer):
        out = []
        for d in range(1, 8):
            nz = lax.rem(z + d, 8)
            nh, nb = z_block(nz)
            src = ub.at[layer, nh, pl.ds(nb, 2)]
            out.append(remote(src, r3.at[layer, d - 1], (s3_send, s3_recv), (layer, d - 1), dev(xl, y, nz, xh)))
        return out

    def z_off(steps):
        return lax.rem(z + steps * (1 - 2 * c) + 8, 8)

    def z_part(layer, nz):
        nh, nb = z_block(nz)
        return summed.at[layer, nh, :, pl.ds(nb, 2), 128:CHUNK, :]

    relays = ((4, 1), (2, 1), (-3, -1))

    def z1_copies(layer):
        out = []
        for k, (to, hop) in enumerate(relays):
            src = z_part(layer, z_off(to))
            out.append(remote(src, rz1.at[layer, k], (z1_send, z1_recv), (layer, k), dev(xl, y, z_off(hop), xh)))
        return out

    def z2_copies(layer):
        out = []
        for k, (to, hop) in enumerate(relays):
            device = dev(xl, y, z_off(to - hop), xh)
            out.append(remote(tz.at[layer, k], rz2.at[layer, k], (z2_send, z2_recv), (layer, k), device))
        src = z_part(layer, z_off(-1))
        out.append(remote(src, rz2.at[layer, 3], (z2_send, z2_recv), (layer, 3), dev(xl, y, z_off(-1), xh)))
        return out

    upper = z // 4
    place = 4 * x + y

    def plane_src(layer, nx, ny):
        return tc.at[layer, nx // 2, lax.rem(upper + nx, 2), rows_at(16 * jnp.minimum(ny, 2), 16), :]

    def plane_copies(layer):
        out = []
        for e in range(1, 16):
            to = lax.rem(place + e, 16)
            nx, ny = to // 4, to % 4
            src = plane_src(layer, nx, ny)
            device = dev(nx % 2, ny, z, nx // 2)
            out.append(remote(src, rp.at[layer, e - 1], (p_send, p_recv), (layer, e - 1), device))
        return out

    def s4_copies(layer):
        out = []
        for e in range(1, 8):
            device = (lax.rem(t + e, 8), r)
            out.append(remote(r4.at[layer, 0], r4.at[layer, e], (s4_send, s4_recv), (layer, e - 1), device))
        return out

    def wide(value):
        return value.astype(F32)

    def start_all(copies):
        for copy in copies:
            copy.start()

    def wait_all(copies):
        for copy in copies:
            copy.wait()

    def stage1(layer):
        for h, bx, b, packed, j0 in pair_blocks:
            pair_copy(layer, h, bx, b, packed, j0).wait()
            own = block_src(layer, packed, j0 + c)[...]
            summed[layer, h, bx, b] = (wide(own) + wide(pair_in[layer, h, bx, b])).astype(BF16)
        start_all(z1_copies(layer))
        start_all(s1_copies(layer))

    def relay(layer):
        wait_all(z1_copies(layer))
        for k, (to, hop) in enumerate(relays):
            own = z_part(layer, z_off(to - hop))[...]
            tz[layer, k] = (wide(own) + wide(rz1[layer, k])).astype(BF16)
        start_all(z2_copies(layer))

    def plane(layer):
        wait_all(z2_copies(layer))
        total = wide(z_part(layer, z)[...])
        for k in range(4):
            total += wide(rz2[layer, k])
        tc[layer] = total.astype(BF16)
        start_all(plane_copies(layer))

    def stage2(layer):
        wait_all(s1_copies(layer))
        own = summed[layer, 0, :, :, rows_at(32 * y, 32), :]
        ta[layer] = (wide(own) + wide(r1a[layer, 0]) + wide(r1a[layer, 1]) + wide(r1a[layer, 2])).astype(BF16)
        own = summed[layer, 1, xh, :, rows_at(64 * xl, 64), :]
        tb[layer] = (wide(own) + wide(r1b[layer, 0]) + wide(r1b[layer, 1]) + wide(r1b[layer, 2])).astype(BF16)
        start_all(s2_copies(layer))

    def stage3(layer):
        wait_all(s2_copies(layer))
        own = ta[layer, xh, :, rows_at(16 * xl, 16), :]
        ub[layer, 0] = (wide(own) + wide(r2a[layer, 0]) + wide(r2a[layer, 1]) + wide(r2a[layer, 2])).astype(BF16)
        own = tb[layer, :, rows_at(16 * y, 16), :]
        ub[layer, 1] = (wide(own) + wide(r2b[layer, 0]) + wide(r2b[layer, 1]) + wide(r2b[layer, 2])).astype(BF16)
        start_all(s3_copies(layer))

    my_half, my_block = z_block(z)
    scale = 1.0 / math.sqrt(TM * 2 * ROWS * W)

    def stage4(layer):
        wait_all(plane_copies(layer))
        total = wide(plane_src(layer, x, y)[...])
        for e in range(15):
            total += wide(rp[layer, e])
        r4[layer, 0, 2] = total.astype(BF16)
        wait_all(s3_copies(layer))
        for k in range(2):
            total = wide(ub[layer, my_half, my_block + k])
            for d in range(7):
                total += wide(r3[layer, d, k])
            r4[layer, 0, k] = total.astype(BF16)
        start_all(s4_copies(layer))

    def unpacked(value):
        return jnp.where(upper == 0, value, pltpu.roll(value, 64, 1))

    def stage5(layer):
        wait_all(s4_copies(layer))
        for e in range(8):
            u = lax.rem(t + 8 - e, 8)
            uy, ux = u % 4, u // 4
            start = jnp.where(my_half == 0, 32 * uy + 16 * ux, 64 * ux + 16 * uy)
            final[rows_at(start, 16), :W] = wide(r4[layer, e, upper]) * scale
            final[rows_at(start, 16), W:] = unpacked(wide(r4[layer, e, 1 - upper]) * scale)
            start = 128 + 16 * jnp.minimum(uy, 2)
            value = wide(r4[layer, e, 2]) * scale

            @pl.when(jnp.logical_and(ux == 0, uy < 3))
            def _(start=start, value=value):
                final[rows_at(start, 16), :W] = value

            @pl.when(jnp.logical_and(ux == 1, uy < 3))
            def _(start=start, value=value):
                final[rows_at(start, 16), W:] = unpacked(value)

        off = 4 * (z % 2) + 2 * xh + c
        for k in range(8):
            @pl.when(off == k)
            def _(k=k):
                k_grad[layer] = final[2 * k : 2 * k + 162, :C]

    stage1(1)
    kernel_terms(0, first_term)
    forward(2)
    relay(1)
    stage1(0)
    stage2(1)
    plane(1)
    wait_slot(2, 0, sibling_slot)
    back_terms(gext, k1, 1, True)
    relay(0)
    stage3(1)
    wait_corners(2)
    back_terms(gext, k1, 0, False)
    back_terms(gext, k1, 2, False)
    for f in range(2):
        _, slope = silu_parts(vext[1, 1, f].astype(F32))
        in_grad[f, 0] = (back_sum(f) * slope).astype(BF16)

    stage2(0)
    plane(0)
    stage4(1)
    stage3(0)
    stage4(0)
    stage5(1)
    stage5(0)

    finish_sends(0, video)
    finish_sends(1, cotangent)
    finish_sends(2, gext.at[0, 1])


def on_device(video_in, kernels, cotangent):
    dma = pltpu.SemaphoreType.DMA
    any_spec = pl.BlockSpec(memory_space=pl.ANY)
    vmem_spec = pl.BlockSpec(memory_space=pltpu.VMEM)
    return pl.pallas_call(
        kernel,
        out_shape=(
            jax.ShapeDtypeStruct((2, 1, C, W), BF16),
            jax.ShapeDtypeStruct((2, 162, C), F32),
        ),
        in_specs=[any_spec] * 3,
        out_specs=(vmem_spec, vmem_spec),
        scratch_shapes=[
            pltpu.VMEM((C, 5184), BF16),
            pltpu.VMEM((C, 5184), BF16),
            pltpu.VMEM((5184, C), BF16),
            pltpu.VMEM((5184, C), BF16),
            pltpu.VMEM((2, 3, 2, C, W), BF16),
            pltpu.VMEM((2, 3, 2, C, W), BF16),
            pltpu.VMEM((2, 3, 2, C, W), BF16),
            pltpu.VMEM((5184, 2 * W), BF16),
            pltpu.VMEM((3 * C, 2 * W), BF16),
            pltpu.VMEM((3 * C, 2 * W), F32),
            pltpu.VMEM((2, C, W), BF16),
            pltpu.VMEM((2, 5184, W), BF16),
            pltpu.VMEM((2, HALF, W), BF16),
            pltpu.VMEM((2, 2, 2, 6, CHUNK, W), BF16),
            pltpu.VMEM((2, 2, 2, 6, CHUNK, W), BF16),
            pltpu.VMEM((2, 3, 2, 6, 32, W), BF16),
            pltpu.VMEM((2, 3, 6, 64, W), BF16),
            pltpu.VMEM((2, 2, 6, 32, W), BF16),
            pltpu.VMEM((2, 6, 64, W), BF16),
            pltpu.VMEM((2, 3, 6, 16, W), BF16),
            pltpu.VMEM((2, 3, 6, 16, W), BF16),
            pltpu.VMEM((2, 2, 6, 16, W), BF16),
            pltpu.VMEM((2, 7, 2, 16, W), BF16),
            pltpu.VMEM((2, 3, 2, 2, 48, W), BF16),
            pltpu.VMEM((2, 3, 2, 2, 48, W), BF16),
            pltpu.VMEM((2, 4, 2, 2, 48, W), BF16),
            pltpu.VMEM((2, 2, 2, 48, W), BF16),
            pltpu.VMEM((2, 15, 16, W), BF16),
            pltpu.VMEM((2, 8, 3, 16, W), BF16),
            pltpu.VMEM((CHUNK, 2 * W), F32),
            dma((4,)),
            dma((3, 5)),
            dma((3, 2, 3)),
            dma((2, 2, 2, 6)),
            dma((2, 2, 2, 6)),
            dma((2, 2, 3)),
            dma((2, 2, 3)),
            dma((2, 2, 3)),
            dma((2, 2, 3)),
            dma((2, 7)),
            dma((2, 7)),
            dma((2, 3)),
            dma((2, 3)),
            dma((2, 4)),
            dma((2, 4)),
            dma((2, 15)),
            dma((2, 15)),
            dma((2, 7)),
            dma((2, 7)),
        ],
        compiler_params=pltpu.CompilerParams(
            collective_id=0, has_side_effects=True, vmem_limit_bytes=56 * 2**20
        ),
        cost_estimate=pl.CostEstimate(flops=2600000000, bytes_accessed=6000000, transcendentals=500000),
    )(video_in.reshape(2, C, W), jnp.swapaxes(kernels, 1, 2), cotangent.reshape(2, C, W))


def solution(mesh):
    return jax.shard_map(
        on_device,
        mesh=mesh,
        in_specs=(P("tm", "rows", None, None), P(), P("tm", "rows", None, None)),
        out_specs=(P("tm", "rows", None, None), P(None, "rows", None)),
        check_vma=False,
    )
```

time: 68.8 us -> 66.1 us (0.961)
  Pallas kernels: 64.1 us -> 61.7 us
    pallas_call x1, Pallas kernels: 64.1 us -> 61.7 us  [on_device(): pl.pallas_call(kernel, out_shape=(jax.ShapeDtypeStruct((2, 1, C, W), BF16...]
where the time goes in v3:
time: 66.1 us; the launch traced here: 65.7 us
  Pallas kernels  61.7 us (93%)
  local copies, waits for them, and re-layouts  3.41 us (5%)
    pallas_call x1, Pallas kernels, on_device(): pl.pallas_call(kernel, out_shape=(jax.ShapeDtypeStruct((2, 1, C, W), BF16...  61.7 us
    pallas_call x1, local copies, waits for them, and re-layouts, on_device(): pl.pallas_call(kernel, out_shape=(jax.ShapeDtypeStruct((2, 1, C, W), BF16...  1.88 us
    unnamed x1, local copies, waits for them, and re-layouts  1.54 us

profile of v3, /device:TPU:2, one launch (start us, length us, event | category | flops | bytes accessed | tf_op | source)
XLA Modules:
  0.0 65.7 jit_solution(11624208141618685643)
XLA Ops:
  0.6 61.7 %shard_map.50 = (bf16[2,1,192,128]{3,2,1,0:T(8,128)(2,1)}, f32[2,162,192]{2,1,0:T(8,128)}) custom-call(bf16[2,192,128]{2,1,0:T(8,128)(2,1)} %bitcast.4, bf16[2,192,5184]{2,1,0:T(8,128)(2,1)} %bitcast.3, bf16[2,192,128]{2,1,0:T(8,128)(2,1)} %bitcast.5), custom_call_target="tpu_custom_call" | custom-call | flops 2600000000 | bytes 6000000 | tf_op jit(solution)/shard_map/pallas_call | solution.py:549
  62.3 1.9 %copy.5 = f32[2,162,192]{2,0,1:T(2,128)} copy(f32[2,162,192]{2,1,0:T(8,128)} %get-tuple-element.3) | data formatting | bytes 497664 | tf_op jit(solution)/shard_map/pallas_call | solution.py:549
  64.2 1.5 %copy.7 = bf16[2,1,192,128]{3,2,1,0:T(8,128)(2,1)} copy(bf16[2,1,192,128]{3,2,1,0:T(8,128)(2,1)} %get-tuple-element.6) | data formatting | bytes 196608

commit v4 on v3

--- a/solution.py
+++ b/solution.py
@@ -101,7 +101,7 @@
     def gets_time(field):
         return has_past if field == 0 else has_future
 
-    def halo_copy(field, which, src=None):
+    def halo_copy(field, which, f, src=None):
         own, side, ext = own_of(field), side_of(field), exts[field]
         time_device = (t + 1, r) if field == 0 else (t - 1, r)
         if which == 0:
@@ -115,10 +115,10 @@
         else:
             src, device, part, row = ext.at[side, 1], (t, sibling_row), side, 2 * c
         return pltpu.make_async_remote_copy(
-            src_ref=src,
-            dst_ref=ext.at[part, row],
-            send_sem=halo_send.at[field, which],
-            recv_sem=halo_recv.at[field, part, row],
+            src_ref=src.at[f],
+            dst_ref=ext.at[part, row, f],
+            send_sem=halo_send.at[field, which, f],
+            recv_sem=halo_recv.at[field, part, row, f],
             device_id=device,
             device_id_type=MESH,
         )
@@ -140,24 +140,34 @@
 
     def start_own(field, src):
         for which in (0, 2, 1):
-            when(sends(field, which), lambda which=which: halo_copy(field, which, src).start())
-
-    def wait_slot(field, part, row):
+            def act(which=which):
+                for f in range(2):
+                    halo_copy(field, which, f, src).start()
+
+            when(sends(field, which), act)
+
+    def wait_piece(field, part, row, f):
         pltpu.make_async_remote_copy(
-            src_ref=exts[field].at[part, row],
-            dst_ref=exts[field].at[part, row],
-            send_sem=halo_send.at[field, 0],
-            recv_sem=halo_recv.at[field, part, row],
+            src_ref=exts[field].at[part, row, f],
+            dst_ref=exts[field].at[part, row, f],
+            send_sem=halo_send.at[field, 0, f],
+            recv_sem=halo_recv.at[field, part, row, f],
             device_id=(t, sibling_row),
             device_id_type=MESH,
         ).wait_recv()
 
+    def wait_slot(field, part, row):
+        for f in range(2):
+            wait_piece(field, part, row, f)
+
     def forward(field):
         own, side = own_of(field), side_of(field)
-        when(has_far, lambda: wait_slot(field, own, far_slot))
-        when(sends(field, 3), lambda: halo_copy(field, 3).start())
-        when(gets_time(field), lambda: wait_slot(field, side, 1))
-        when(sends(field, 4), lambda: halo_copy(field, 4).start())
+        for f in range(2):
+            when(has_far, lambda: wait_piece(field, own, far_slot, f))
+            when(sends(field, 3), lambda: halo_copy(field, 3, f).start())
+        for f in range(2):
+            when(gets_time(field), lambda: wait_piece(field, side, 1, f))
+            when(sends(field, 4), lambda: halo_copy(field, 4, f).start())
 
     def wait_corners(field):
         side = side_of(field)
@@ -166,7 +176,11 @@
 
     def finish_sends(field, src):
         for which in range(5):
-            when(sends(field, which), lambda which=which: halo_copy(field, which, src).wait_send())
+            def act(which=which):
+                for f in range(2):
+                    halo_copy(field, which, f, src).wait_send()
+
+            when(sends(field, which), act)
 
     start_own(0, video)
     start_own(1, cotangent)
@@ -203,6 +217,30 @@
             n = min(W, 5184 - start)
             dst[start : start + n, :] = jnp.transpose(src[:, start : start + n])
 
+    def field_pair(ext, tt, p):
+        at = (2 - tt, 3 - tt)
+        return jnp.concatenate([ext[a // 2, 2 - p, a % 2] for a in at], axis=1)
+
+    EARLY = [(2, 1), (2, 0), (2, 2), (1, 1), (0, 1)]
+    LATE = [(1, 0), (1, 2), (0, 0), (0, 2)]
+
+    def back_terms(ext, k_ref, taps, first):
+        for tt, p in taps:
+            g = tt * 3 + p
+            term = dot(k_ref[g * 576 : (g + 1) * 576, :], field_pair(ext, tt, p))
+            if first and (tt, p) == taps[0]:
+                acc[...] = term
+            else:
+                acc[...] += term
+
+    def back_sum(f):
+        cols = slice(f * W, (f + 1) * W)
+        return (
+            lane_shift(acc[0:C, cols], -1)
+            + acc[C : 2 * C, cols]
+            + lane_shift(acc[2 * C : 3 * C, cols], 1)
+        )
+
     loads[0].wait()
     activate(1, 1)
     loads[3].wait()
@@ -214,24 +252,28 @@
     wait_slot(0, 1, sibling_slot)
     activate(1, 0)
     activate(1, 2)
+    late = dot(k1t[:, 3456:], stack[3456:, :])
     forward(1)
-    late = dot(k1t[:, 3456:], stack[3456:, :])
+    loads[1].wait()
+    wait_slot(1, 0, sibling_slot)
+    back_terms(cext, k2, EARLY, True)
     wait_corners(0)
     activate(0, 0)
     activate(0, 2)
     out = late + dot(k1t[:, :3456], stack[:3456, :])
     for f in range(2):
-        x1[f] = out[:, f * W : (f + 1) * W].astype(BF16)
+        value = out[:, f * W : (f + 1) * W].astype(BF16)
+        x1[f] = value
+        value, _ = silu_parts(value.astype(F32))
+        shifted = (lane_shift(value, 1), value, lane_shift(value, -1))
+        for q in range(3):
+            acts2[q * C : (q + 1) * C, f * W : (f + 1) * W] = shifted[q].astype(BF16)
 
     zeros64 = jnp.zeros((64, 2 * W), BF16)
 
     def widened(value, upper):
         lo, hi = value[:W], value[W:C]
         return jnp.concatenate([lo, zeros64, hi] if upper else [lo, hi, zeros64], axis=0)
-
-    def field_pair(ext, tt, p):
-        at = (2 - tt, 3 - tt)
-        return jnp.concatenate([ext[a // 2, 2 - p, a % 2] for a in at], axis=1)
 
     pair_blocks = []
     for h in range(2):
@@ -241,9 +283,11 @@
                 z_to = 2 * h + zi + (4 if kind == 2 else 0)
                 pair_blocks.append((h, bx, b, kind == 1, 4 * z_to + 2 * bx))
 
-    def ready_at(block):
-        j = block[4] % 16 + 1
-        return -(-(16 * ((81 * j) // 8) + CHUNK) // 288) - 1
+    def steps_of(block):
+        j = block[4] % 16
+        first = 16 * ((81 * j) // 8)
+        last = 16 * ((81 * (j + 1)) // 8) + CHUNK - 1
+        return set(range(first // 288, last // 288 + 1))
 
     def block_src(layer, packed, j):
         ref = wb if packed else wa
@@ -261,56 +305,35 @@
             device_id_type=MESH,
         )
 
-    def kernel_terms(layer, term):
-        for k in range(9):
-            at = 288 * k
-            low, high = term(k, False), term(k + 9, True)
-            wa[layer, at : at + 288, :] = low[:, :W].astype(BF16)
-            wa[layer, HALF + at : HALF + at + 288, :] = high[:, :W].astype(BF16)
-            wb[layer, at : at + 288, :] = (low[:, W:] + high[:, W:]).astype(BF16)
+    def kernel_terms(layer, term, order, done, sent):
+        for hg in order:
+            k, at = hg % 9, 288 * hg
+            value = term(hg, hg >= 9)
+            wa[layer, at : at + 288, :] = value[:, :W].astype(BF16)
+            rest = value[:, W:].astype(BF16)
+            if (hg + 9) % 18 in done:
+                wb[layer, 288 * k : 288 * k + 288, :] += rest
+            else:
+                wb[layer, 288 * k : 288 * k + 288, :] = rest
+            done.add(hg)
             for block in pair_blocks:
-                if ready_at(block) == k:
+                if block not in sent and all(n in done and n + 9 in done for n in steps_of(block)):
+                    sent.add(block)
                     pair_copy(layer, *block).start()
-
-    def back_terms(ext, k_ref, p, first):
-        for tt in range(3):
-            g = tt * 3 + p
-            term = dot(k_ref[g * 576 : (g + 1) * 576, :], field_pair(ext, tt, p))
-            if first and tt == 0:
-                acc[...] = term
-            else:
-                acc[...] += term
-
-    def back_sum(f):
-        cols = slice(f * W, (f + 1) * W)
-        return (
-            lane_shift(acc[0:C, cols], -1)
-            + acc[C : 2 * C, cols]
-            + lane_shift(acc[2 * C : 3 * C, cols], 1)
-        )
-
-    for f in range(2):
-        value, _ = silu_parts(x1[f].astype(F32))
-        shifted = (lane_shift(value, 1), value, lane_shift(value, -1))
-        for q in range(3):
-            acts2[q * C : (q + 1) * C, f * W : (f + 1) * W] = shifted[q].astype(BF16)
-    loads[1].wait()
-    wait_slot(1, 0, sibling_slot)
-    wait_corners(1)
 
     def second_term(hg, upper):
         g, part = hg // 2, hg % 2
         pair = widened(field_pair(cext, g // 3, g % 3), upper)
         return dot_nt(acts2[288 * part : 288 * part + 288, :], pair)
 
-    kernel_terms(1, second_term)
-
-    for p in range(3):
-        back_terms(cext, k2, p, p == 0)
+    done, sent = set(), set()
+    kernel_terms(1, second_term, [9, 12, 3, 13, 14, 15, 16, 17, 8, 2], done, sent)
+    wait_corners(1)
+    kernel_terms(1, second_term, [0, 1, 10, 11, 4, 5, 6, 7], done, sent)
+    back_terms(cext, k2, LATE, False)
     for f in range(2):
         _, slope = silu_parts(x1[f].astype(F32))
         gext[0, 1, f] = (back_sum(f) * slope).astype(BF16)
-    start_own(2, gext.at[0, 1])
 
     def first_term(hg, upper):
         pair = jnp.concatenate([gext[0, 1, 0], gext[0, 1, 1]], axis=1)
@@ -428,12 +451,14 @@
             copy.wait()
 
     def stage1(layer):
-        for h, bx, b, packed, j0 in pair_blocks:
-            pair_copy(layer, h, bx, b, packed, j0).wait()
-            own = block_src(layer, packed, j0 + c)[...]
-            summed[layer, h, bx, b] = (wide(own) + wide(pair_in[layer, h, bx, b])).astype(BF16)
+        copies = s1_copies(layer)
+        for half in range(2):
+            for h, bx, b, packed, j0 in pair_blocks:
+                if h == half:
+                    pair_copy(layer, h, bx, b, packed, j0).wait()
+                    summed[layer, h, bx, b] = block_src(layer, packed, j0 + c)[...] + pair_in[layer, h, bx, b]
+            start_all(copies[half::2])
         start_all(z1_copies(layer))
-        start_all(s1_copies(layer))
 
     def relay(layer):
         wait_all(z1_copies(layer))
@@ -512,27 +537,27 @@
                 k_grad[layer] = final[2 * k : 2 * k + 162, :C]
 
     stage1(1)
-    kernel_terms(0, first_term)
+    kernel_terms(0, first_term, [n for k in range(9) for n in (k, k + 9)], set(), set())
+    stage1(0)
+    start_own(2, gext.at[0, 1])
+    relay(1)
+    stage2(1)
+    relay(0)
+    stage2(0)
+    plane(1)
+    stage3(1)
     forward(2)
-    relay(1)
-    stage1(0)
-    stage2(1)
-    plane(1)
+    plane(0)
+    stage3(0)
     wait_slot(2, 0, sibling_slot)
-    back_terms(gext, k1, 1, True)
-    relay(0)
-    stage3(1)
+    back_terms(gext, k1, EARLY, True)
+    stage4(1)
     wait_corners(2)
-    back_terms(gext, k1, 0, False)
-    back_terms(gext, k1, 2, False)
+    back_terms(gext, k1, LATE, False)
     for f in range(2):
         _, slope = silu_parts(vext[1, 1, f].astype(F32))
         in_grad[f, 0] = (back_sum(f) * slope).astype(BF16)
 
-    stage2(0)
-    plane(0)
-    stage4(1)
-    stage3(0)
     stage4(0)
     stage5(1)
     stage5(0)
@@ -586,8 +611,8 @@
             pltpu.VMEM((2, 8, 3, 16, W), BF16),
             pltpu.VMEM((CHUNK, 2 * W), F32),
             dma((4,)),
-            dma((3, 5)),
-            dma((3, 2, 3)),
+            dma((3, 5, 2)),
+            dma((3, 2, 3, 2)),
             dma((2, 2, 2, 6)),
             dma((2, 2, 2, 6)),
             dma((2, 2, 3)),

time: 66.1 us -> 61.3 us (0.927); the launches traced: 65.7 us -> 60.2 us
  Pallas kernels: 61.7 us -> 56.1 us
    pallas_call x1, Pallas kernels: 61.7 us -> 56.1 us  [on_device(): pl.pallas_call(kernel, out_shape=(jax.ShapeDtypeStruct((2, 1, C, W), BF16...]
where the time goes in v4:
time: 61.3 us; the launch traced here: 60.2 us
  Pallas kernels  56.1 us (92%)
  local copies, waits for them, and re-layouts  3.41 us (6%)
  between operations  0.64 us (1%)
    pallas_call x1, Pallas kernels, on_device(): pl.pallas_call(kernel, out_shape=(jax.ShapeDtypeStruct((2, 1, C, W), BF16...  56.1 us
    pallas_call x1, local copies, waits for them, and re-layouts, on_device(): pl.pallas_call(kernel, out_shape=(jax.ShapeDtypeStruct((2, 1, C, W), BF16...  1.88 us
    unnamed x1, local copies, waits for them, and re-layouts  1.54 us

profile of v4, /device:TPU:2, one launch (start us, length us, event | category | flops | bytes accessed | tf_op | source)
XLA Modules:
  0.0 60.2 jit_solution(2966257847353500771)
XLA Ops:
  0.6 56.1 %shard_map.50 = (bf16[2,1,192,128]{3,2,1,0:T(8,128)(2,1)}, f32[2,162,192]{2,1,0:T(8,128)}) custom-call(bf16[2,192,128]{2,1,0:T(8,128)(2,1)} %bitcast.4, bf16[2,192,5184]{2,1,0:T(8,128)(2,1)} %bitcast.3, bf16[2,192,128]{2,1,0:T(8,128)(2,1)} %bitcast.5), custom_call_target="tpu_custom_call" | custom-call | flops 2600000000 | bytes 6000000 | tf_op jit(solution)/shard_map/pallas_call | solution.py:574
  56.8 1.9 %copy.5 = f32[2,162,192]{2,0,1:T(2,128)} copy(f32[2,162,192]{2,1,0:T(8,128)} %get-tuple-element.3) | data formatting | bytes 497664 | tf_op jit(solution)/shard_map/pallas_call | solution.py:574
  58.7 1.5 %copy.7 = bf16[2,1,192,128]{3,2,1,0:T(8,128)(2,1)} copy(bf16[2,1,192,128]{3,2,1,0:T(8,128)(2,1)} %get-tuple-element.6) | data formatting | bytes 196608

commit v5 on v4

--- a/solution.py
+++ b/solution.py
@@ -14,7 +14,6 @@
 W = 128
 TM = 8
 ROWS = 32
-HALF = 2592
 CHUNK = 176
 
 
@@ -44,9 +43,9 @@
 
 def kernel(
     video, kernels, cotangent, in_grad, k_grad,
-    k1t, k2t, k1, k2, vext, cext, gext, stack, acts2, acc, x1, wa, wb, pair_in, summed,
+    k1t, k2t, k1, k2, vext, cext, gext, stack, a2, acts2, acc, x1, summed,
     r1a, r1b, ta, tb, r2a, r2b, ub, r3, rz1, tz, rz2, tc, rp, r4, final,
-    load_sem, halo_send, halo_recv, pair_send, pair_recv,
+    load_sem, halo_send, halo_recv, a2_sem,
     s1_send, s1_recv, s2_send, s2_recv, s3_send, s3_recv, z1_send, z1_recv, z2_send, z2_recv,
     p_send, p_recv, s4_send, s4_recv,
 ):
@@ -57,12 +56,13 @@
     x = 2 * xh + xl
     has_far = jnp.logical_and(r > 0, r < ROWS - 1)
     far_row, sibling_row = r - 1 + 2 * c, r + 1 - 2 * c
-    far_slot, sibling_slot = 2 * c, 2 - 2 * c
+    me, sib, far, sib_far = 1 + c, 2 - c, 3 * c, 3 - 3 * c
+    sib_has_far = jnp.logical_and(sibling_row > 0, sibling_row < ROWS - 1)
     has_past, has_future = t > 0, t < TM - 1
 
     loads = [
-        pltpu.make_async_copy(video, vext.at[1, 1], load_sem.at[0]),
-        pltpu.make_async_copy(cotangent, cext.at[0, 1], load_sem.at[1]),
+        pltpu.make_async_copy(video, vext.at[1, me], load_sem.at[0]),
+        pltpu.make_async_copy(cotangent, cext.at[0, me], load_sem.at[1]),
         pltpu.make_async_copy(kernels.at[0], k1t, load_sem.at[2]),
         pltpu.make_async_copy(kernels.at[1], k2t, load_sem.at[3]),
     ]
@@ -104,16 +104,19 @@
     def halo_copy(field, which, f, src=None):
         own, side, ext = own_of(field), side_of(field), exts[field]
         time_device = (t + 1, r) if field == 0 else (t - 1, r)
-        if which == 0:
-            device, part, row = (t, far_row), own, 2 - 2 * c
-        elif which == 1:
-            device, part, row = (t, sibling_row), own, 2 * c
-        elif which == 2:
-            device, part, row = time_device, side, 1
-        elif which == 3:
-            src, device, part, row = ext.at[own, far_slot], time_device, side, far_slot
-        else:
-            src, device, part, row = ext.at[side, 1], (t, sibling_row), side, 2 * c
+        part, row, device = (
+            (own, sib_far, (t, far_row)),
+            (own, me, (t, sibling_row)),
+            (side, me, time_device),
+            (side, far, time_device),
+            (side, me, (t, sibling_row)),
+            (own, far, (t, sibling_row)),
+            (side, far, (t, sibling_row)),
+        )[which]
+        if which == 3:
+            src = ext.at[own, far]
+        elif which > 3:
+            src = ext.at[part, row]
         return pltpu.make_async_remote_copy(
             src_ref=src.at[f],
             dst_ref=ext.at[part, row, f],
@@ -130,6 +133,8 @@
             sends_time(field),
             jnp.logical_and(has_far, sends_time(field)),
             gets_time(field),
+            has_far,
+            jnp.logical_and(has_far, gets_time(field)),
         )[which]
 
     def when(cond, act):
@@ -138,13 +143,16 @@
         else:
             pl.when(cond)(act)
 
+    def start_halo(field, which, src=None):
+        def act():
+            for f in range(2):
+                halo_copy(field, which, f, src).start()
+
+        when(sends(field, which), act)
+
     def start_own(field, src):
         for which in (0, 2, 1):
-            def act(which=which):
-                for f in range(2):
-                    halo_copy(field, which, f, src).start()
-
-            when(sends(field, which), act)
+            start_halo(field, which, src)
 
     def wait_piece(field, part, row, f):
         pltpu.make_async_remote_copy(
@@ -156,26 +164,42 @@
             device_id_type=MESH,
         ).wait_recv()
 
-    def wait_slot(field, part, row):
-        for f in range(2):
-            wait_piece(field, part, row, f)
+    def wait_block(field, part, row, cond=None):
+        def act():
+            for f in range(2):
+                wait_piece(field, part, row, f)
+
+        when(cond, act)
 
     def forward(field):
         own, side = own_of(field), side_of(field)
         for f in range(2):
-            when(has_far, lambda: wait_piece(field, own, far_slot, f))
+            when(has_far, lambda: wait_piece(field, own, far, f))
             when(sends(field, 3), lambda: halo_copy(field, 3, f).start())
+        if field < 2:
+            start_halo(field, 5)
         for f in range(2):
-            when(gets_time(field), lambda: wait_piece(field, side, 1, f))
+            when(gets_time(field), lambda: wait_piece(field, side, me, f))
             when(sends(field, 4), lambda: halo_copy(field, 4, f).start())
+
+    def wait_sibling(field):
+        wait_block(field, own_of(field), sib)
 
     def wait_corners(field):
         side = side_of(field)
-        when(jnp.logical_and(has_far, gets_time(field)), lambda: wait_slot(field, side, far_slot))
-        when(gets_time(field), lambda: wait_slot(field, side, sibling_slot))
+        wait_block(field, side, far, jnp.logical_and(has_far, gets_time(field)))
+        if field < 2:
+            start_halo(field, 6)
+        wait_block(field, side, sib, gets_time(field))
+
+    def wait_sibling_far(field, corner):
+        if corner:
+            wait_block(field, side_of(field), sib_far, jnp.logical_and(sib_has_far, gets_time(field)))
+        else:
+            wait_block(field, own_of(field), sib_far, sib_has_far)
 
     def finish_sends(field, src):
-        for which in range(5):
+        for which in range(7 if field < 2 else 5):
             def act(which=which):
                 for f in range(2):
                     halo_copy(field, which, f, src).wait_send()
@@ -193,13 +217,22 @@
     for field in range(3):
         own, side = own_of(field), side_of(field)
         no_time = jnp.logical_not(gets_time(field))
-        no_far = jnp.logical_not(has_far)
-        when(no_far, lambda: clear(field, own, far_slot))
-        when(no_time, lambda: clear(field, side, 1))
-        when(no_time, lambda: clear(field, side, sibling_slot))
-        when(jnp.logical_or(no_time, no_far), lambda: clear(field, side, far_slot))
-
-    def activate(part, row):
+        for row, has in ((far, has_far), (sib_far, sib_has_far)):
+            none = jnp.logical_not(has)
+            when(none, lambda: clear(field, own, row))
+            when(jnp.logical_or(no_time, none), lambda: clear(field, side, row))
+        for row in (me, sib):
+            when(no_time, lambda: clear(field, side, row))
+
+    enters = {
+        "me": (me, ((c, 1), (1 - c, 2 * c))),
+        "sib": (sib, ((c, 2 - 2 * c), (1 - c, 1))),
+        "far": (far, ((c, 2 * c),)),
+        "sib_far": (sib_far, ((1 - c, 2 - 2 * c),)),
+    }
+
+    def activate(part, name):
+        row, targets = enters[name]
         for f in range(2):
             at = 2 * part + f
             value, _ = silu_parts(vext[part, row, f].astype(F32))
@@ -209,17 +242,18 @@
                 for to in range(2):
                     tt = at - to
                     if 0 <= tt <= 2:
-                        start = (tt * 9 + row * 3 + q) * C
-                        stack[start : start + C, to * W : (to + 1) * W] = block
+                        for center, p in targets:
+                            start = pl.multiple_of((tt * 9 + q) * C + p * 3 * C, 16)
+                            stack[center, pl.ds(start, C), to * W : (to + 1) * W] = block
 
     def turn(src, dst):
         for start in range(0, 5184, W):
             n = min(W, 5184 - start)
             dst[start : start + n, :] = jnp.transpose(src[:, start : start + n])
 
-    def field_pair(ext, tt, p):
+    def field_pair(ext, tt, p, center):
         at = (2 - tt, 3 - tt)
-        return jnp.concatenate([ext[a // 2, 2 - p, a % 2] for a in at], axis=1)
+        return jnp.concatenate([ext[a // 2, center + 1 - p, a % 2] for a in at], axis=1)
 
     EARLY = [(2, 1), (2, 0), (2, 2), (1, 1), (0, 1)]
     LATE = [(1, 0), (1, 2), (0, 0), (0, 2)]
@@ -227,7 +261,7 @@
     def back_terms(ext, k_ref, taps, first):
         for tt, p in taps:
             g = tt * 3 + p
-            term = dot(k_ref[g * 576 : (g + 1) * 576, :], field_pair(ext, tt, p))
+            term = dot(k_ref[g * 576 : (g + 1) * 576, :], field_pair(ext, tt, p, me))
             if first and (tt, p) == taps[0]:
                 acc[...] = term
             else:
@@ -241,103 +275,103 @@
             + lane_shift(acc[2 * C : 3 * C, cols], 1)
         )
 
+    zeros64 = jnp.zeros((64, 2 * W), BF16)
+
+    def widened(value, upper):
+        lo, hi = value[:W], value[W:C]
+        return jnp.concatenate([lo, zeros64, hi] if upper else [lo, hi, zeros64], axis=0)
+
+    def put(layer, m, bx, low, high):
+        h, b = m // 2, 3 * (m % 2)
+        summed[layer, h, bx, b] = low[:, :W].astype(BF16)
+        summed[layer, h, bx, b + 1] = (low[:, W:] + high[:, W:]).astype(BF16)
+        summed[layer, h, bx, b + 2] = high[:, :W].astype(BF16)
+
+    def second_chunk(j, upper):
+        start, pieces = 16 * ((81 * j) // 8), []
+        at = start
+        while at < start + CHUNK:
+            g = at // 576
+            n = min(start + CHUNK, 576 * (g + 1)) - at
+            rhs = [widened(field_pair(cext, g // 3, g % 3, center), upper) for center in (1, 2)]
+            pieces.append(dot_nt(acts2[at - 576 * g : at - 576 * g + n, :], jnp.concatenate(rhs, axis=1)))
+            at += n
+        return pieces[0] if len(pieces) == 1 else jnp.concatenate(pieces, axis=0)
+
+    def second_terms(planes):
+        for core in range(2):
+            @pl.when(c == core)
+            def _(core=core):
+                for m in planes:
+                    for bx in range(2):
+                        j = 8 * m + 2 * bx + core
+                        put(1, m, bx, second_chunk(j, False), second_chunk(j + 4, True))
+
+    def first_terms(planes):
+        rows = [jnp.concatenate([gext[0, center, 0], gext[0, center, 1]], axis=1) for center in (1, 2)]
+        rhs = [jnp.concatenate([widened(v, upper) for v in rows], axis=1) for upper in (False, True)]
+        for m in planes:
+            for bx in range(2):
+                out = []
+                for upper in range(2):
+                    at = pl.ds(chunk_start(8 * m + 4 * upper + 2 * bx + c), CHUNK)
+                    out.append(dot_nt(jnp.concatenate([stack[0, at, :], stack[1, at, :]], axis=1), rhs[upper]))
+                put(0, m, bx, *out)
+
     loads[0].wait()
-    activate(1, 1)
+    activate(1, "me")
     loads[3].wait()
     turn(k2t, k2)
     loads[2].wait()
     turn(k1t, k1)
     forward(0)
-    activate(0, 1)
-    wait_slot(0, 1, sibling_slot)
-    activate(1, 0)
-    activate(1, 2)
-    late = dot(k1t[:, 3456:], stack[3456:, :])
+    activate(0, "me")
+    activate(1, "far")
+    wait_sibling(0)
+    activate(1, "sib")
+    late = dot(k1t[:, 3456:], stack[c, 3456:, :])
     forward(1)
     loads[1].wait()
-    wait_slot(1, 0, sibling_slot)
+    wait_sibling(1)
     back_terms(cext, k2, EARLY, True)
     wait_corners(0)
-    activate(0, 0)
-    activate(0, 2)
-    out = late + dot(k1t[:, :3456], stack[:3456, :])
+    activate(0, "far")
+    activate(0, "sib")
+    out = late + dot(k1t[:, :3456], stack[c, :3456, :])
     for f in range(2):
         value = out[:, f * W : (f + 1) * W].astype(BF16)
         x1[f] = value
         value, _ = silu_parts(value.astype(F32))
-        shifted = (lane_shift(value, 1), value, lane_shift(value, -1))
-        for q in range(3):
-            acts2[q * C : (q + 1) * C, f * W : (f + 1) * W] = shifted[q].astype(BF16)
-
-    zeros64 = jnp.zeros((64, 2 * W), BF16)
-
-    def widened(value, upper):
-        lo, hi = value[:W], value[W:C]
-        return jnp.concatenate([lo, zeros64, hi] if upper else [lo, hi, zeros64], axis=0)
-
-    pair_blocks = []
-    for h in range(2):
-        for bx in range(2):
-            for b in range(6):
-                zi, kind = b // 3, b % 3
-                z_to = 2 * h + zi + (4 if kind == 2 else 0)
-                pair_blocks.append((h, bx, b, kind == 1, 4 * z_to + 2 * bx))
-
-    def steps_of(block):
-        j = block[4] % 16
-        first = 16 * ((81 * j) // 8)
-        last = 16 * ((81 * (j + 1)) // 8) + CHUNK - 1
-        return set(range(first // 288, last // 288 + 1))
-
-    def block_src(layer, packed, j):
-        ref = wb if packed else wa
-        return ref.at[layer, pl.ds(chunk_start(j), CHUNK), :]
-
-    sibling = (t, sibling_row)
-
-    def pair_copy(layer, h, bx, b, packed, j0):
-        return pltpu.make_async_remote_copy(
-            src_ref=block_src(layer, packed, j0 + 1 - c),
-            dst_ref=pair_in.at[layer, h, bx, b],
-            send_sem=pair_send.at[layer, h, bx, b],
-            recv_sem=pair_recv.at[layer, h, bx, b],
-            device_id=sibling,
-            device_id_type=MESH,
-        )
-
-    def kernel_terms(layer, term, order, done, sent):
-        for hg in order:
-            k, at = hg % 9, 288 * hg
-            value = term(hg, hg >= 9)
-            wa[layer, at : at + 288, :] = value[:, :W].astype(BF16)
-            rest = value[:, W:].astype(BF16)
-            if (hg + 9) % 18 in done:
-                wb[layer, 288 * k : 288 * k + 288, :] += rest
-            else:
-                wb[layer, 288 * k : 288 * k + 288, :] = rest
-            done.add(hg)
-            for block in pair_blocks:
-                if block not in sent and all(n in done and n + 9 in done for n in steps_of(block)):
-                    sent.add(block)
-                    pair_copy(layer, *block).start()
-
-    def second_term(hg, upper):
-        g, part = hg // 2, hg % 2
-        pair = widened(field_pair(cext, g // 3, g % 3), upper)
-        return dot_nt(acts2[288 * part : 288 * part + 288, :], pair)
-
-    done, sent = set(), set()
-    kernel_terms(1, second_term, [9, 12, 3, 13, 14, 15, 16, 17, 8, 2], done, sent)
+        a2[c, f] = value.astype(BF16)
+    a2_copy = pltpu.make_async_remote_copy(
+        src_ref=a2.at[c],
+        dst_ref=a2.at[c],
+        send_sem=a2_sem.at[0],
+        recv_sem=a2_sem.at[1],
+        device_id=(t, sibling_row),
+        device_id_type=MESH,
+    )
+    a2_copy.start()
+    wait_sibling_far(0, False)
+    activate(1, "sib_far")
+    wait_sibling_far(1, False)
+    a2_copy.wait_recv()
+    for center in range(2):
+        for f in range(2):
+            value = a2[center, f].astype(F32)
+            shifted = (lane_shift(value, 1), value, lane_shift(value, -1))
+            cols = slice((2 * center + f) * W, (2 * center + f + 1) * W)
+            for q in range(3):
+                acts2[q * C : (q + 1) * C, cols] = shifted[q].astype(BF16)
+    second_terms([3])
     wait_corners(1)
-    kernel_terms(1, second_term, [0, 1, 10, 11, 4, 5, 6, 7], done, sent)
     back_terms(cext, k2, LATE, False)
     for f in range(2):
         _, slope = silu_parts(x1[f].astype(F32))
-        gext[0, 1, f] = (back_sum(f) * slope).astype(BF16)
-
-    def first_term(hg, upper):
-        pair = jnp.concatenate([gext[0, 1, 0], gext[0, 1, 1]], axis=1)
-        return dot_nt(stack[288 * hg : 288 * hg + 288, :], widened(pair, upper))
+        gext[0, me, f] = (back_sum(f) * slope).astype(BF16)
+    start_halo(2, 1, gext.at[0, me])
+    wait_sibling_far(1, True)
+    second_terms([2, 0, 1])
 
     def dev(nxl, ny, nz, nxh):
         return (nxl * 4 + ny, nz * 4 + nxh * 2 + c)
@@ -356,7 +390,7 @@
         return pl.ds(pl.multiple_of(start, 16), n)
 
     def z_block(nz):
-        return (nz % 4) // 2, 3 * (nz % 2) + nz // 4
+        return nz // 4, 3 * ((nz // 2) % 2) + nz % 2
 
     def s1_copies(layer):
         out = []
@@ -416,7 +450,7 @@
         out.append(remote(src, rz2.at[layer, 3], (z2_send, z2_recv), (layer, 3), dev(xl, y, z_off(-1), xh)))
         return out
 
-    upper = z // 4
+    upper = z % 2
     place = 4 * x + y
 
     def plane_src(layer, nx, ny):
@@ -451,13 +485,7 @@
             copy.wait()
 
     def stage1(layer):
-        copies = s1_copies(layer)
-        for half in range(2):
-            for h, bx, b, packed, j0 in pair_blocks:
-                if h == half:
-                    pair_copy(layer, h, bx, b, packed, j0).wait()
-                    summed[layer, h, bx, b] = block_src(layer, packed, j0 + c)[...] + pair_in[layer, h, bx, b]
-            start_all(copies[half::2])
+        start_all(s1_copies(layer))
         start_all(z1_copies(layer))
 
     def relay(layer):
@@ -537,9 +565,13 @@
                 k_grad[layer] = final[2 * k : 2 * k + 162, :C]
 
     stage1(1)
-    kernel_terms(0, first_term, [n for k in range(9) for n in (k, k + 9)], set(), set())
+    wait_sibling_far(0, True)
+    activate(0, "sib_far")
+    wait_sibling(2)
+    first_terms(range(4))
     stage1(0)
-    start_own(2, gext.at[0, 1])
+    start_halo(2, 0, gext.at[0, me])
+    start_halo(2, 2, gext.at[0, me])
     relay(1)
     stage2(1)
     relay(0)
@@ -549,13 +581,12 @@
     forward(2)
     plane(0)
     stage3(0)
-    wait_slot(2, 0, sibling_slot)
     back_terms(gext, k1, EARLY, True)
     stage4(1)
     wait_corners(2)
     back_terms(gext, k1, LATE, False)
     for f in range(2):
-        _, slope = silu_parts(vext[1, 1, f].astype(F32))
+        _, slope = silu_parts(vext[1, me, f].astype(F32))
         in_grad[f, 0] = (back_sum(f) * slope).astype(BF16)
 
     stage4(0)
@@ -564,14 +595,21 @@
 
     finish_sends(0, video)
     finish_sends(1, cotangent)
-    finish_sends(2, gext.at[0, 1])
+    finish_sends(2, gext.at[0, me])
+    a2_copy.wait_send()
+
+
+def finish(in_src, k_src, in_dst, k_dst):
+    in_dst[:, 0] = in_src[:, 0]
+    for layer in range(2):
+        k_dst[:, layer, :] = k_src[layer]
 
 
 def on_device(video_in, kernels, cotangent):
     dma = pltpu.SemaphoreType.DMA
     any_spec = pl.BlockSpec(memory_space=pl.ANY)
     vmem_spec = pl.BlockSpec(memory_space=pltpu.VMEM)
-    return pl.pallas_call(
+    in_grad, k_grad = pl.pallas_call(
         kernel,
         out_shape=(
             jax.ShapeDtypeStruct((2, 1, C, W), BF16),
@@ -584,16 +622,14 @@
             pltpu.VMEM((C, 5184), BF16),
             pltpu.VMEM((5184, C), BF16),
             pltpu.VMEM((5184, C), BF16),
-            pltpu.VMEM((2, 3, 2, C, W), BF16),
-            pltpu.VMEM((2, 3, 2, C, W), BF16),
-            pltpu.VMEM((2, 3, 2, C, W), BF16),
-            pltpu.VMEM((5184, 2 * W), BF16),
-            pltpu.VMEM((3 * C, 2 * W), BF16),
+            pltpu.VMEM((2, 4, 2, C, W), BF16),
+            pltpu.VMEM((2, 4, 2, C, W), BF16),
+            pltpu.VMEM((2, 4, 2, C, W), BF16),
+            pltpu.VMEM((2, 5184, 2 * W), BF16),
+            pltpu.VMEM((2, 2, C, W), BF16),
+            pltpu.VMEM((3 * C, 4 * W), BF16),
             pltpu.VMEM((3 * C, 2 * W), F32),
             pltpu.VMEM((2, C, W), BF16),
-            pltpu.VMEM((2, 5184, W), BF16),
-            pltpu.VMEM((2, HALF, W), BF16),
-            pltpu.VMEM((2, 2, 2, 6, CHUNK, W), BF16),
             pltpu.VMEM((2, 2, 2, 6, CHUNK, W), BF16),
             pltpu.VMEM((2, 3, 2, 6, 32, W), BF16),
             pltpu.VMEM((2, 3, 6, 64, W), BF16),
@@ -611,10 +647,9 @@
             pltpu.VMEM((2, 8, 3, 16, W), BF16),
             pltpu.VMEM((CHUNK, 2 * W), F32),
             dma((4,)),
-            dma((3, 5, 2)),
-            dma((3, 2, 3, 2)),
-            dma((2, 2, 2, 6)),
-            dma((2, 2, 2, 6)),
+            dma((3, 7, 2)),
+            dma((3, 2, 4, 2)),
+            dma((2,)),
             dma((2, 2, 3)),
             dma((2, 2, 3)),
             dma((2, 2, 3)),
@@ -635,6 +670,16 @@
         ),
         cost_estimate=pl.CostEstimate(flops=2600000000, bytes_accessed=6000000, transcendentals=500000),
     )(video_in.reshape(2, C, W), jnp.swapaxes(kernels, 1, 2), cotangent.reshape(2, C, W))
+    in_grad, k_grad = pl.pallas_call(
+        finish,
+        out_shape=(
+            jax.ShapeDtypeStruct((2, 1, C, W), BF16),
+            jax.ShapeDtypeStruct((162, 2, C), F32),
+        ),
+        in_specs=[vmem_spec, vmem_spec],
+        out_specs=(vmem_spec, vmem_spec),
+    )(in_grad, k_grad)
+    return in_grad, jnp.swapaxes(k_grad, 0, 1)
 
 
 def solution(mesh):

time: 61.3 us -> 58 us (0.946); the launches traced: 60.2 us -> 57.9 us
  local copies, waits for them, and re-layouts: 3.41 us -> 0 us
  Pallas kernels: 56.1 us -> 57.3 us
    pallas_call x1 -> x0, local copies, waits for them, and re-layouts: 1.88 us -> none  [on_device(): pl.pallas_call(kernel, out_shape=(jax.ShapeDtypeStruct((2, 1, C, W), BF16...]
    pallas_call x0 -> x1, Pallas kernels: none -> 1.87 us  [on_device(): pl.pallas_call(finish, out_shape=(jax.ShapeDtypeStruct((2, 1, C, W), BF16...]
    unnamed x1 -> x0, local copies, waits for them, and re-layouts: 1.54 us -> none
    pallas_call x1, Pallas kernels: 56.1 us -> 55.4 us  [on_device(): pl.pallas_call(kernel, out_shape=(jax.ShapeDtypeStruct((2, 1, C, W), BF16...]
where the time goes in v5:
time: 58 us; the launch traced here: 57.9 us
  Pallas kernels  57.3 us (99%)
  between operations  0.64 us (1%)
    pallas_call x1, Pallas kernels, on_device(): pl.pallas_call(kernel, out_shape=(jax.ShapeDtypeStruct((2, 1, C, W), BF16...  55.4 us
    pallas_call x1, Pallas kernels, on_device(): pl.pallas_call(finish, out_shape=(jax.ShapeDtypeStruct((2, 1, C, W), BF16...  1.87 us

profile of v5, /device:TPU:2, one launch (start us, length us, event | category | flops | bytes accessed | tf_op | source)
XLA Modules:
  0.0 57.9 jit_solution(10206986788787305796)
XLA Ops:
  0.6 55.4 %shard_map.50 = (bf16[2,1,192,128]{3,2,1,0:T(8,128)(2,1)}, f32[2,162,192]{2,1,0:T(8,128)}) custom-call(bf16[2,192,128]{2,1,0:T(8,128)(2,1)} %bitcast.6, bf16[2,192,5184]{2,1,0:T(8,128)(2,1)} %bitcast.4, bf16[2,192,128]{2,1,0:T(8,128)(2,1)} %bitcast.7), custom_call_target="tpu_custom_call" | custom-call | flops 2600000000 | bytes 6000000 | tf_op jit(solution)/shard_map/pallas_call | solution.py:612
  56.1 1.9 %shard_map.51 = (bf16[2,1,192,128]{3,2,1,0:T(8,128)(2,1)}, f32[162,2,192]{2,1,0:T(2,128)}) custom-call(bf16[2,1,192,128]{3,2,1,0:T(8,128)(2,1)} %get-tuple-element.6.in_src, f32[2,162,192]{2,1,0:T(8,128)} %get-tuple-element.7.k_src), custom_call_target="tpu_custom_call" | custom-call | tf_op jit(solution)/shard_map/pallas_call | solution.py:673

commit v6 on v5

--- a/solution.py
+++ b/solution.py
@@ -317,6 +317,198 @@
                     at = pl.ds(chunk_start(8 * m + 4 * upper + 2 * bx + c), CHUNK)
                     out.append(dot_nt(jnp.concatenate([stack[0, at, :], stack[1, at, :]], axis=1), rhs[upper]))
                 put(0, m, bx, *out)
+
+    def dev(nxl, ny, nz, nxh):
+        return (nxl * 4 + ny, nz * 4 + nxh * 2 + c)
+
+    def remote(src, dst, sems, at, device):
+        return pltpu.make_async_remote_copy(
+            src_ref=src,
+            dst_ref=dst,
+            send_sem=sems[0].at[at],
+            recv_sem=sems[1].at[at],
+            device_id=device,
+            device_id_type=MESH,
+        )
+
+    def rows_at(start, n):
+        return pl.ds(pl.multiple_of(start, 16), n)
+
+    def z_block(nz):
+        return nz // 4, 3 * ((nz // 2) % 2) + nz % 2
+
+    def s1_copies(layer, halves=(0, 1)):
+        out = []
+        for d in (2, 1, 3):
+            if 0 in halves:
+                ny = lax.rem(y + d, 4)
+                src = summed.at[layer, 0, :, :, rows_at(32 * ny, 32), :]
+                out.append(
+                    remote(src, r1a.at[layer, d - 1], (s1_send, s1_recv), (layer, 0, d - 1), dev(xl, ny, z, xh))
+                )
+            if 1 in halves:
+                nx = lax.rem(x + d, 4)
+                src = summed.at[layer, 1, nx // 2, :, rows_at(64 * (nx % 2), 64), :]
+                out.append(
+                    remote(src, r1b.at[layer, d - 1], (s1_send, s1_recv), (layer, 1, d - 1), dev(nx % 2, y, z, nx // 2))
+                )
+        return out
+
+    def s2_copies(layer):
+        out = []
+        for d in (2, 1, 3):
+            ny, nx = lax.rem(y + d, 4), lax.rem(x + d, 4)
+            src = ta.at[layer, nx // 2, :, rows_at(16 * (nx % 2), 16), :]
+            out.append(
+                remote(src, r2a.at[layer, d - 1], (s2_send, s2_recv), (layer, 0, d - 1), dev(nx % 2, y, z, nx // 2))
+            )
+            src = tb.at[layer, :, rows_at(16 * ny, 16), :]
+            out.append(remote(src, r2b.at[layer, d - 1], (s2_send, s2_recv), (layer, 1, d - 1), dev(xl, ny, z, xh)))
+        return out
+
+    def s3_copies(layer):
+        out = []
+        for d in (4, 3, 5, 2, 6, 1, 7):
+            nz = lax.rem(z + d, 8)
+            nh, nb = z_block(nz)
+            src = ub.at[layer, nh, pl.ds(nb, 2)]
+            out.append(remote(src, r3.at[layer, d - 1], (s3_send, s3_recv), (layer, d - 1), dev(xl, y, nz, xh)))
+        return out
+
+    def z_off(steps):
+        return lax.rem(z + steps * (1 - 2 * c) + 8, 8)
+
+    def z_part(layer, nz):
+        nh, nb = z_block(nz)
+        return summed.at[layer, nh, :, pl.ds(nb, 2), 128:CHUNK, :]
+
+    relays = ((4, 1), (2, 1), (-3, -1))
+
+    def z1_copies(layer):
+        out = []
+        for k, (to, hop) in enumerate(relays):
+            src = z_part(layer, z_off(to))
+            out.append(remote(src, rz1.at[layer, k], (z1_send, z1_recv), (layer, k), dev(xl, y, z_off(hop), xh)))
+        return out
+
+    def z2_copies(layer):
+        out = []
+        for k, (to, hop) in enumerate(relays):
+            device = dev(xl, y, z_off(to - hop), xh)
+            out.append(remote(tz.at[layer, k], rz2.at[layer, k], (z2_send, z2_recv), (layer, k), device))
+        src = z_part(layer, z_off(-1))
+        out.append(remote(src, rz2.at[layer, 3], (z2_send, z2_recv), (layer, 3), dev(xl, y, z_off(-1), xh)))
+        return out
+
+    upper = z % 2
+    place = 4 * x + y
+
+    def plane_src(layer, nx, ny):
+        return tc.at[layer, nx // 2, lax.rem(upper + nx, 2), rows_at(16 * jnp.minimum(ny, 2), 16), :]
+
+    def plane_copies(layer):
+        out = []
+        for e in (10, 9, 11, 6, 14, 8, 2, 5, 7, 13, 15, 4, 12, 1, 3):
+            to = lax.rem(place + e, 16)
+            nx, ny = to // 4, to % 4
+            src = plane_src(layer, nx, ny)
+            device = dev(nx % 2, ny, z, nx // 2)
+            out.append(remote(src, rp.at[layer, e - 1], (p_send, p_recv), (layer, e - 1), device))
+        return out
+
+    def s4_copies(layer):
+        out = []
+        for e in range(1, 8):
+            device = (lax.rem(t + e, 8), r)
+            out.append(remote(r4.at[layer, 0], r4.at[layer, e], (s4_send, s4_recv), (layer, e - 1), device))
+        return out
+
+    def wide(value):
+        return value.astype(F32)
+
+    def start_all(copies):
+        for copy in copies:
+            copy.start()
+
+    def wait_all(copies):
+        for copy in copies:
+            copy.wait()
+
+    def relay(layer):
+        wait_all(z1_copies(layer))
+        for k, (to, hop) in enumerate(relays):
+            own = z_part(layer, z_off(to - hop))[...]
+            tz[layer, k] = (wide(own) + wide(rz1[layer, k])).astype(BF16)
+        start_all(z2_copies(layer))
+
+    def plane(layer):
+        wait_all(z2_copies(layer))
+        total = wide(z_part(layer, z)[...])
+        for k in range(4):
+            total += wide(rz2[layer, k])
+        tc[layer] = total.astype(BF16)
+        start_all(plane_copies(layer))
+
+    def stage2(layer):
+        wait_all(s1_copies(layer))
+        own = summed[layer, 0, :, :, rows_at(32 * y, 32), :]
+        ta[layer] = (wide(own) + wide(r1a[layer, 0]) + wide(r1a[layer, 1]) + wide(r1a[layer, 2])).astype(BF16)
+        own = summed[layer, 1, xh, :, rows_at(64 * xl, 64), :]
+        tb[layer] = (wide(own) + wide(r1b[layer, 0]) + wide(r1b[layer, 1]) + wide(r1b[layer, 2])).astype(BF16)
+        start_all(s2_copies(layer))
+
+    def stage3(layer):
+        wait_all(s2_copies(layer))
+        own = ta[layer, xh, :, rows_at(16 * xl, 16), :]
+        ub[layer, 0] = (wide(own) + wide(r2a[layer, 0]) + wide(r2a[layer, 1]) + wide(r2a[layer, 2])).astype(BF16)
+        own = tb[layer, :, rows_at(16 * y, 16), :]
+        ub[layer, 1] = (wide(own) + wide(r2b[layer, 0]) + wide(r2b[layer, 1]) + wide(r2b[layer, 2])).astype(BF16)
+        start_all(s3_copies(layer))
+
+    my_half, my_block = z_block(z)
+    scale = 1.0 / math.sqrt(TM * 2 * ROWS * W)
+
+    def stage4(layer):
+        wait_all(plane_copies(layer))
+        total = wide(plane_src(layer, x, y)[...])
+        for e in range(15):
+            total += wide(rp[layer, e])
+        r4[layer, 0, 2] = total.astype(BF16)
+        wait_all(s3_copies(layer))
+        for k in range(2):
+            total = wide(ub[layer, my_half, my_block + k])
+            for d in range(7):
+                total += wide(r3[layer, d, k])
+            r4[layer, 0, k] = total.astype(BF16)
+        start_all(s4_copies(layer))
+
+    def unpacked(value):
+        return jnp.where(upper == 0, value, pltpu.roll(value, 64, 1))
+
+    def stage5(layer):
+        wait_all(s4_copies(layer))
+        for e in range(8):
+            u = lax.rem(t + 8 - e, 8)
+            uy, ux = u % 4, u // 4
+            start = jnp.where(my_half == 0, 32 * uy + 16 * ux, 64 * ux + 16 * uy)
+            final[rows_at(start, 16), :W] = wide(r4[layer, e, upper]) * scale
+            final[rows_at(start, 16), W:] = unpacked(wide(r4[layer, e, 1 - upper]) * scale)
+            start = 128 + 16 * jnp.minimum(uy, 2)
+            value = wide(r4[layer, e, 2]) * scale
+
+            @pl.when(jnp.logical_and(ux == 0, uy < 3))
+            def _(start=start, value=value):
+                final[rows_at(start, 16), :W] = value
+
+            @pl.when(jnp.logical_and(ux == 1, uy < 3))
+            def _(start=start, value=value):
+                final[rows_at(start, 16), W:] = unpacked(value)
+
+        off = 4 * (z % 2) + 2 * xh + c
+        for k in range(8):
+            @pl.when(off == k)
+            def _(k=k):
+                k_grad[layer] = final[2 * k : 2 * k + 162, :C]
 
     loads[0].wait()
     activate(1, "me")
@@ -371,228 +563,42 @@
         gext[0, me, f] = (back_sum(f) * slope).astype(BF16)
     start_halo(2, 1, gext.at[0, me])
     wait_sibling_far(1, True)
-    second_terms([2, 0, 1])
-
-    def dev(nxl, ny, nz, nxh):
-        return (nxl * 4 + ny, nz * 4 + nxh * 2 + c)
-
-    def remote(src, dst, sems, at, device):
-        return pltpu.make_async_remote_copy(
-            src_ref=src,
-            dst_ref=dst,
-            send_sem=sems[0].at[at],
-            recv_sem=sems[1].at[at],
-            device_id=device,
-            device_id_type=MESH,
-        )
-
-    def rows_at(start, n):
-        return pl.ds(pl.multiple_of(start, 16), n)
-
-    def z_block(nz):
-        return nz // 4, 3 * ((nz // 2) % 2) + nz % 2
-
-    def s1_copies(layer):
-        out = []
-        for d in range(1, 4):
-            ny, nx = lax.rem(y + d, 4), lax.rem(x + d, 4)
-            src = summed.at[layer, 0, :, :, rows_at(32 * ny, 32), :]
-            out.append(remote(src, r1a.at[layer, d - 1], (s1_send, s1_recv), (layer, 0, d - 1), dev(xl, ny, z, xh)))
-            src = summed.at[layer, 1, nx // 2, :, rows_at(64 * (nx % 2), 64), :]
-            out.append(
-                remote(src, r1b.at[layer, d - 1], (s1_send, s1_recv), (layer, 1, d - 1), dev(nx % 2, y, z, nx // 2))
-            )
-        return out
-
-    def s2_copies(layer):
-        out = []
-        for d in range(1, 4):
-            ny, nx = lax.rem(y + d, 4), lax.rem(x + d, 4)
-            src = ta.at[layer, nx // 2, :, rows_at(16 * (nx % 2), 16), :]
-            out.append(
-                remote(src, r2a.at[layer, d - 1], (s2_send, s2_recv), (layer, 0, d - 1), dev(nx % 2, y, z, nx // 2))
-            )
-            src = tb.at[layer, :, rows_at(16 * ny, 16), :]
-            out.append(remote(src, r2b.at[layer, d - 1], (s2_send, s2_recv), (layer, 1, d - 1), dev(xl, ny, z, xh)))
-        return out
-
-    def s3_copies(layer):
-        out = []
-        for d in range(1, 8):
-            nz = lax.rem(z + d, 8)
-            nh, nb = z_block(nz)
-            src = ub.at[layer, nh, pl.ds(nb, 2)]
-            out.append(remote(src, r3.at[layer, d - 1], (s3_send, s3_recv), (layer, d - 1), dev(xl, y, nz, xh)))
-        return out
-
-    def z_off(steps):
-        return lax.rem(z + steps * (1 - 2 * c) + 8, 8)
-
-    def z_part(layer, nz):
-        nh, nb = z_block(nz)
-        return summed.at[layer, nh, :, pl.ds(nb, 2), 128:CHUNK, :]
-
-    relays = ((4, 1), (2, 1), (-3, -1))
-
-    def z1_copies(layer):
-        out = []
-        for k, (to, hop) in enumerate(relays):
-            src = z_part(layer, z_off(to))
-            out.append(remote(src, rz1.at[layer, k], (z1_send, z1_recv), (layer, k), dev(xl, y, z_off(hop), xh)))
-        return out
-
-    def z2_copies(layer):
-        out = []
-        for k, (to, hop) in enumerate(relays):
-            device = dev(xl, y, z_off(to - hop), xh)
-            out.append(remote(tz.at[layer, k], rz2.at[layer, k], (z2_send, z2_recv), (layer, k), device))
-        src = z_part(layer, z_off(-1))
-        out.append(remote(src, rz2.at[layer, 3], (z2_send, z2_recv), (layer, 3), dev(xl, y, z_off(-1), xh)))
-        return out
-
-    upper = z % 2
-    place = 4 * x + y
-
-    def plane_src(layer, nx, ny):
-        return tc.at[layer, nx // 2, lax.rem(upper + nx, 2), rows_at(16 * jnp.minimum(ny, 2), 16), :]
-
-    def plane_copies(layer):
-        out = []
-        for e in range(1, 16):
-            to = lax.rem(place + e, 16)
-            nx, ny = to // 4, to % 4
-            src = plane_src(layer, nx, ny)
-            device = dev(nx % 2, ny, z, nx // 2)
-            out.append(remote(src, rp.at[layer, e - 1], (p_send, p_recv), (layer, e - 1), device))
-        return out
-
-    def s4_copies(layer):
-        out = []
-        for e in range(1, 8):
-            device = (lax.rem(t + e, 8), r)
-            out.append(remote(r4.at[layer, 0], r4.at[layer, e], (s4_send, s4_recv), (layer, e - 1), device))
-        return out
-
-    def wide(value):
-        return value.astype(F32)
-
-    def start_all(copies):
-        for copy in copies:
-            copy.start()
-
-    def wait_all(copies):
-        for copy in copies:
-            copy.wait()
-
-    def stage1(layer):
-        start_all(s1_copies(layer))
-        start_all(z1_copies(layer))
-
-    def relay(layer):
-        wait_all(z1_copies(layer))
-        for k, (to, hop) in enumerate(relays):
-            own = z_part(layer, z_off(to - hop))[...]
-            tz[layer, k] = (wide(own) + wide(rz1[layer, k])).astype(BF16)
-        start_all(z2_copies(layer))
-
-    def plane(layer):
-        wait_all(z2_copies(layer))
-        total = wide(z_part(layer, z)[...])
-        for k in range(4):
-            total += wide(rz2[layer, k])
-        tc[layer] = total.astype(BF16)
-        start_all(plane_copies(layer))
-
-    def stage2(layer):
-        wait_all(s1_copies(layer))
-        own = summed[layer, 0, :, :, rows_at(32 * y, 32), :]
-        ta[layer] = (wide(own) + wide(r1a[layer, 0]) + wide(r1a[layer, 1]) + wide(r1a[layer, 2])).astype(BF16)
-        own = summed[layer, 1, xh, :, rows_at(64 * xl, 64), :]
-        tb[layer] = (wide(own) + wide(r1b[layer, 0]) + wide(r1b[layer, 1]) + wide(r1b[layer, 2])).astype(BF16)
-        start_all(s2_copies(layer))
-
-    def stage3(layer):
-        wait_all(s2_copies(layer))
-        own = ta[layer, xh, :, rows_at(16 * xl, 16), :]
-        ub[layer, 0] = (wide(own) + wide(r2a[layer, 0]) + wide(r2a[layer, 1]) + wide(r2a[layer, 2])).astype(BF16)
-        own = tb[layer, :, rows_at(16 * y, 16), :]
-        ub[layer, 1] = (wide(own) + wide(r2b[layer, 0]) + wide(r2b[layer, 1]) + wide(r2b[layer, 2])).astype(BF16)
-        start_all(s3_copies(layer))
-
-    my_half, my_block = z_block(z)
-    scale = 1.0 / math.sqrt(TM * 2 * ROWS * W)
-
-    def stage4(layer):
-        wait_all(plane_copies(layer))
-        total = wide(plane_src(layer, x, y)[...])
-        for e in range(15):
-            total += wide(rp[layer, e])
-        r4[layer, 0, 2] = total.astype(BF16)
-        wait_all(s3_copies(layer))
-        for k in range(2):
-            total = wide(ub[layer, my_half, my_block + k])
-            for d in range(7):
-                total += wide(r3[layer, d, k])
-            r4[layer, 0, k] = total.astype(BF16)
-        start_all(s4_copies(layer))
-
-    def unpacked(value):
-        return jnp.where(upper == 0, value, pltpu.roll(value, 64, 1))
-
-    def stage5(layer):
-        wait_all(s4_copies(layer))
-        for e in range(8):
-            u = lax.rem(t + 8 - e, 8)
-            uy, ux = u % 4, u // 4
-            start = jnp.where(my_half == 0, 32 * uy + 16 * ux, 64 * ux + 16 * uy)
-            final[rows_at(start, 16), :W] = wide(r4[layer, e, upper]) * scale
-            final[rows_at(start, 16), W:] = unpacked(wide(r4[layer, e, 1 - upper]) * scale)
-            start = 128 + 16 * jnp.minimum(uy, 2)
-            value = wide(r4[layer, e, 2]) * scale
-
-            @pl.when(jnp.logical_and(ux == 0, uy < 3))
-            def _(start=start, value=value):
-                final[rows_at(start, 16), :W] = value
-
-            @pl.when(jnp.logical_and(ux == 1, uy < 3))
-            def _(start=start, value=value):
-                final[rows_at(start, 16), W:] = unpacked(value)
-
-        off = 4 * (z % 2) + 2 * xh + c
-        for k in range(8):
-            @pl.when(off == k)
-            def _(k=k):
-                k_grad[layer] = final[2 * k : 2 * k + 162, :C]
-
-    stage1(1)
+    second_terms([2])
+    start_all(s1_copies(1, (1,)))
+    second_terms([0, 1])
+    start_all(s1_copies(1, (0,)))
+    start_all(z1_copies(1))
+
     wait_sibling_far(0, True)
     activate(0, "sib_far")
     wait_sibling(2)
-    first_terms(range(4))
-    stage1(0)
-    start_halo(2, 0, gext.at[0, me])
-    start_halo(2, 2, gext.at[0, me])
+    first_terms((2, 3))
+    start_all(s1_copies(0, (1,)))
+    first_terms((0, 1))
+    start_all(s1_copies(0, (0,)))
+    start_all(z1_copies(0))
     relay(1)
     stage2(1)
     relay(0)
     stage2(0)
+    start_halo(2, 0, gext.at[0, me])
+    start_halo(2, 2, gext.at[0, me])
     plane(1)
     stage3(1)
-    forward(2)
     plane(0)
     stage3(0)
+    forward(2)
     back_terms(gext, k1, EARLY, True)
     stage4(1)
+    stage4(0)
     wait_corners(2)
     back_terms(gext, k1, LATE, False)
     for f in range(2):
         _, slope = silu_parts(vext[1, me, f].astype(F32))
         in_grad[f, 0] = (back_sum(f) * slope).astype(BF16)
 
-    stage4(0)
     stage5(1)
     stage5(0)
-
     finish_sends(0, video)
     finish_sends(1, cotangent)
     finish_sends(2, gext.at[0, me])

time: 58 us -> 56.1 us (0.967)
  Pallas kernels: 57.3 us -> 55.3 us
    pallas_call x1, Pallas kernels: 55.4 us -> 53.5 us  [on_device(): pl.pallas_call(kernel, out_shape=(jax.ShapeDtypeStruct((2, 1, C, W), BF16...]
where the time goes in v6:
time: 56.1 us; the launch traced here: 56 us
  Pallas kernels  55.3 us (99%)
  between operations  0.64 us (1%)
    pallas_call x1, Pallas kernels, on_device(): pl.pallas_call(kernel, out_shape=(jax.ShapeDtypeStruct((2, 1, C, W), BF16...  53.5 us
    pallas_call x1, Pallas kernels, on_device(): pl.pallas_call(finish, out_shape=(jax.ShapeDtypeStruct((2, 1, C, W), BF16...  1.87 us

profile of v6, /device:TPU:2, one launch (start us, length us, event | category | flops | bytes accessed | tf_op | source)
XLA Modules:
  0.0 56.0 jit_solution(4187813912531283793)
XLA Ops:
  0.6 53.5 %shard_map.50 = (bf16[2,1,192,128]{3,2,1,0:T(8,128)(2,1)}, f32[2,162,192]{2,1,0:T(8,128)}) custom-call(bf16[2,192,128]{2,1,0:T(8,128)(2,1)} %bitcast.6, bf16[2,192,5184]{2,1,0:T(8,128)(2,1)} %bitcast.4, bf16[2,192,128]{2,1,0:T(8,128)(2,1)} %bitcast.7), custom_call_target="tpu_custom_call" | custom-call | flops 2600000000 | bytes 6000000 | tf_op jit(solution)/shard_map/pallas_call | solution.py:618
  54.1 1.9 %shard_map.51 = (bf16[2,1,192,128]{3,2,1,0:T(8,128)(2,1)}, f32[162,2,192]{2,1,0:T(2,128)}) custom-call(bf16[2,1,192,128]{3,2,1,0:T(8,128)(2,1)} %get-tuple-element.6.in_src, f32[2,162,192]{2,1,0:T(8,128)} %get-tuple-element.7.k_src), custom_call_target="tpu_custom_call" | custom-call | tf_op jit(solution)/shard_map/pallas_call | solution.py:679

commit v7 on v6

--- a/solution.py
+++ b/solution.py
@@ -44,7 +44,7 @@
 def kernel(
     video, kernels, cotangent, in_grad, k_grad,
     k1t, k2t, k1, k2, vext, cext, gext, stack, a2, acts2, acc, x1, summed,
-    r1a, r1b, ta, tb, r2a, r2b, ub, r3, rz1, tz, rz2, tc, rp, r4, final,
+    r1a, r1b, ta, tb, r2a, r2b, ub, r3, rz1, tz, rz2, tc, rp, r4,
     load_sem, halo_send, halo_recv, a2_sem,
     s1_send, s1_recv, s2_send, s2_recv, s3_send, s3_recv, z1_send, z1_recv, z2_send, z2_recv,
     p_send, p_recv, s4_send, s4_recv,
@@ -491,24 +491,18 @@
             u = lax.rem(t + 8 - e, 8)
             uy, ux = u % 4, u // 4
             start = jnp.where(my_half == 0, 32 * uy + 16 * ux, 64 * ux + 16 * uy)
-            final[rows_at(start, 16), :W] = wide(r4[layer, e, upper]) * scale
-            final[rows_at(start, 16), W:] = unpacked(wide(r4[layer, e, 1 - upper]) * scale)
+            k_grad[layer, rows_at(start, 16), :W] = wide(r4[layer, e, upper]) * scale
+            k_grad[layer, rows_at(start, 16), W:] = unpacked(wide(r4[layer, e, 1 - upper]) * scale)
             start = 128 + 16 * jnp.minimum(uy, 2)
             value = wide(r4[layer, e, 2]) * scale
 
             @pl.when(jnp.logical_and(ux == 0, uy < 3))
             def _(start=start, value=value):
-                final[rows_at(start, 16), :W] = value
+                k_grad[layer, rows_at(start, 16), :W] = value
 
             @pl.when(jnp.logical_and(ux == 1, uy < 3))
             def _(start=start, value=value):
-                final[rows_at(start, 16), W:] = unpacked(value)
-
-        off = 4 * (z % 2) + 2 * xh + c
-        for k in range(8):
-            @pl.when(off == k)
-            def _(k=k):
-                k_grad[layer] = final[2 * k : 2 * k + 162, :C]
+                k_grad[layer, rows_at(start, 16), W:] = unpacked(value)
 
     loads[0].wait()
     activate(1, "me")
@@ -607,8 +601,12 @@
 
 def finish(in_src, k_src, in_dst, k_dst):
     in_dst[:, 0] = in_src[:, 0]
-    for layer in range(2):
-        k_dst[:, layer, :] = k_src[layer]
+    off = lax.axis_index("rows") % 8
+    for k in range(8):
+        @pl.when(off == k)
+        def _(k=k):
+            for layer in range(2):
+                k_dst[:, layer, :] = k_src[layer, 2 * k : 2 * k + 162, :C]
 
 
 def on_device(video_in, kernels, cotangent):
@@ -619,7 +617,7 @@
         kernel,
         out_shape=(
             jax.ShapeDtypeStruct((2, 1, C, W), BF16),
-            jax.ShapeDtypeStruct((2, 162, C), F32),
+            jax.ShapeDtypeStruct((2, CHUNK, 2 * W), F32),
         ),
         in_specs=[any_spec] * 3,
         out_specs=(vmem_spec, vmem_spec),
@@ -651,7 +649,6 @@
             pltpu.VMEM((2, 2, 2, 48, W), BF16),
             pltpu.VMEM((2, 15, 16, W), BF16),
             pltpu.VMEM((2, 8, 3, 16, W), BF16),
-            pltpu.VMEM((CHUNK, 2 * W), F32),
             dma((4,)),
             dma((3, 7, 2)),
             dma((3, 2, 4, 2)),

time: 56.1 us -> 56.1 us (level)
  no operation moved by 1% of the time
where the time goes in v7:
time: 56.1 us; the launch traced here: 56 us
  Pallas kernels  55.3 us (99%)
  between operations  0.64 us (1%)
    pallas_call x1, Pallas kernels, on_device(): pl.pallas_call(kernel, out_shape=(jax.ShapeDtypeStruct((2, 1, C, W), BF16...  53.4 us
    pallas_call x1, Pallas kernels, on_device(): pl.pallas_call(finish, out_shape=(jax.ShapeDtypeStruct((2, 1, C, W), BF16...  1.94 us

profile of v7, /device:TPU:2, one launch (start us, length us, event | category | flops | bytes accessed | tf_op | source)
XLA Modules:
  0.0 56.0 jit_solution(12688647188055941921)
XLA Ops:
  0.6 53.4 %shard_map.50 = (bf16[2,1,192,128]{3,2,1,0:T(8,128)(2,1)}, f32[2,176,256]{2,1,0:T(8,128)}) custom-call(bf16[2,192,128]{2,1,0:T(8,128)(2,1)} %bitcast.6, bf16[2,192,5184]{2,1,0:T(8,128)(2,1)} %bitcast.4, bf16[2,192,128]{2,1,0:T(8,128)(2,1)} %bitcast.7), custom_call_target="tpu_custom_call" | custom-call | flops 2600000000 | bytes 6000000 | tf_op jit(solution)/shard_map/pallas_call | solution.py:616
  54.0 1.9 %shard_map.51 = (bf16[2,1,192,128]{3,2,1,0:T(8,128)(2,1)}, f32[162,2,192]{2,1,0:T(2,128)}) custom-call(bf16[2,1,192,128]{3,2,1,0:T(8,128)(2,1)} %get-tuple-element.6.in_src, f32[2,176,256]{2,1,0:T(8,128)} %get-tuple-element.7.k_src), custom_call_target="tpu_custom_call" | custom-call | tf_op jit(solution)/shard_map/pallas_call | solution.py:676
